TPU v7x, 256 devices: a whole 4x4x8 slice. The times are simulated.
256 devices in a mesh: batch: 64 (over y, z_lo, x), rep: 4 (over z_hi, core).
Axes of the slice: x: 4, y: 4, z: 8 (z_hi: 2, z_lo: 4; z = z_hi * 4 + z_lo), core: 2. Of those that a mesh axis runs over, the one named last changes fastest.
Arguments:
- images: bfloat16 [65536, 1152], P(('batch', 'rep')), may hold values from -0.41015625 to 0.41015625
- caption_vectors: bfloat16 [65536, 1152], P(('batch', 'rep')), may hold values from -0.41015625 to 0.41015625
- sample_weight: float32 [65536], P(('batch', 'rep')), may hold values from 0.4 to 22.5, as said below
- natural_odds_factor: float32 [1], replicated, may hold values from 1.6 to 2.8
- bias: float32 [1], replicated, may hold values from -3 to -1
Outputs:
- loss: float32 [1], replicated
- grad_scalars: float32 [2], replicated
- grad_images: bfloat16 [65536, 1152], P(('batch', 'rep'))
- grad_texts: bfloat16 [65536, 1152], P(('batch', 'rep'))
Inputs may be any that keep to these rules, and one draw needn't show every extreme that they name: `sample_weight`: positive weights.
All inputs are finite; a program needn't handle non-finite values.
Results may differ from a plain program's by a relative error of at most 0.017.
Values may be sent and summed in bfloat16 or wider, within the bound.
No kernel may reach another device: no remote copies, remote signals or barrier semaphores. Data moves between devices by JAX's collectives and lax.ppermute only.
A program may use at most 128 MiB of HBM per device.

v0:
```python
import jax
import jax.numpy as jnp
from jax import lax
from jax.sharding import PartitionSpec as P

ROUNDS = 3


def swapped(value, axis, stride):
    mask = 2**stride
    pairs = [(source, source ^ mask) for source in range(lax.axis_size(axis))]
    return lax.ppermute(value, axis, pairs)


def block_loss_terms(
    picture_line_group,
    caption_line_group,
    example_importance,
    odds_sharpness,
    line_start_shift,
    matching_indicator,
):
    couple_similarity = lax.dot_general(
        picture_line_group,
        caption_line_group,
        (((1,), (1,)), ((), ())),
        preferred_element_type=jnp.float32,
    )
    couple_odds = odds_sharpness * couple_similarity + line_start_shift
    importance_similarity = example_importance[:, None] * (
        jax.nn.sigmoid(couple_odds) - matching_indicator
    )
    couple_strength = importance_similarity.astype(jnp.bfloat16)
    subtotal_penalty = jnp.sum(
        example_importance[:, None]
        * (jax.nn.softplus(couple_odds) - matching_indicator * couple_odds)
    )
    return (
        couple_strength,
        (
            subtotal_penalty,
            odds_sharpness * jnp.sum(importance_similarity * couple_similarity),
            jnp.sum(importance_similarity),
        ),
    )


def first_factor_multiply(couple_strength, picture_line_group, odds_sharpness):
    return odds_sharpness * lax.dot_general(
        couple_strength,
        picture_line_group,
        (((0,), (0,)), ((), ())),
        preferred_element_type=jnp.float32,
    )


def send_back(caption_portion, flipped):
    return swapped(caption_portion, "batch", flipped)


def settle(partial_results):
    return lax.psum((partial_results[0], partial_results[1], partial_results[2]), ("batch", "rep"))


def add_up(earlier, later):
    return tuple((former + latter for former, latter in zip(earlier, later)))


def on_device(images, caption_vectors, sample_weight, natural_odds_factor, bias):
    row_count = images.shape[0]
    rep_count = lax.axis_size("rep")
    rep_index = lax.axis_index("rep")
    groups = lax.axis_size("batch")
    bit_width = groups.bit_length() - 1
    odds_sharpness = jnp.exp(natural_odds_factor[0])
    line_start_shift = bias[0]
    blank_outcome = jnp.float32(0.0)
    totals = (blank_outcome, blank_outcome, blank_outcome)
    partner_bits = [step_index * (bit_width - 1) // (ROUNDS - 1) for step_index in range(ROUNDS)]
    group_rows = row_count * rep_count
    own_pictures, own_importance = (
        lax.all_gather(images, "rep", axis=0, tiled=True),
        lax.all_gather(sample_weight.astype(jnp.bfloat16), "rep", axis=0, tiled=True).astype(
            sample_weight.dtype
        ),
    )
    row_ids = lax.broadcasted_iota(jnp.int32, (group_rows, row_count), 0)
    col_ids = lax.broadcasted_iota(jnp.int32, (group_rows, row_count), 1)
    matching_indicator = (row_ids == col_ids + rep_index * row_count).astype(jnp.float32)
    couple_strength, partial_results = block_loss_terms(
        own_pictures,
        caption_vectors,
        own_importance,
        odds_sharpness,
        line_start_shift,
        matching_indicator,
    )
    picture_derivative_sum = odds_sharpness * jnp.dot(
        couple_strength, caption_vectors, preferred_element_type=jnp.float32
    )
    own_portion = first_factor_multiply(couple_strength, own_pictures, odds_sharpness).astype(
        jnp.bfloat16
    )
    text_total = lax.optimization_barrier(own_portion).astype(jnp.float32)
    totals = add_up(totals, settle(partial_results))
    for flipped in partner_bits:
        fourth_number = swapped(caption_vectors, "batch", flipped)
        couple_strength, partial_results = block_loss_terms(
            own_pictures,
            fourth_number,
            own_importance,
            odds_sharpness,
            line_start_shift,
            blank_outcome,
        )
        picture_derivative_sum = picture_derivative_sum + odds_sharpness * jnp.dot(
            couple_strength, fourth_number, preferred_element_type=jnp.float32
        )
        caption_portion = first_factor_multiply(
            couple_strength, own_pictures, odds_sharpness
        ).astype(jnp.bfloat16)
        text_total = text_total + send_back(caption_portion, flipped).astype(jnp.float32)
        totals = add_up(totals, settle(partial_results))
    picture_derivative = lax.psum_scatter(
        picture_derivative_sum.astype(jnp.bfloat16), "rep", scatter_dimension=0, tiled=True
    )
    pair_count = float(group_rows * groups * group_rows * (ROUNDS + 1))
    loss = jnp.reshape(totals[0] / pair_count, (1,))
    grad_scalars = jnp.stack([totals[1], totals[2]]) / pair_count
    return (loss, grad_scalars, picture_derivative, text_total.astype(jnp.bfloat16))


def solution(mesh):
    in_specs = (P(("batch", "rep"), None), P(("batch", "rep"), None), P(("batch", "rep")), P(), P())
    out_specs = (P(), P(), P(("batch", "rep"), None), P(("batch", "rep"), None))
    return jax.shard_map(
        on_device, mesh=mesh, in_specs=in_specs, out_specs=out_specs, check_vma=False
    )
```

profile of v0, /device:TPU:1, one launch (start us, length us, event | category | flops | bytes accessed | tf_op | source)
XLA Modules:
  0.0 190.2 jit_solution(13368829818930850591)
XLA Ops:
  7.2 0.7 all-gather.3.cloned.1.call-update
  7.9 2.1 %collective-permute-start = (bf16[256,1152]{1,0:T(8,128)(2,1)}, bf16[256,1152]{1,0:T(8,128)(2,1)S(1)}, u32[]{:S(2)}, u32[]{:S(2)}) collective-permute-start(bf16[256,1152]{1,0:T(8,128)(2,1)} %param.6), channel_id=1, source_target_pairs={{0,4},{4,0},{8,12},{12,8},{16,20},{20,16},{24,28},{28,24},{32,36},... | collective-permute-start | bytes 1769480 | tf_op jit(solution)/shard_map/ppermute | solution.py:12
  10.1 1.6 collective-permute-start.1
  11.7 2.9 %collective-permute-start.2 = (bf16[256,1152]{1,0:T(8,128)(2,1)}, bf16[256,1152]{1,0:T(8,128)(2,1)}, u32[]{:S(2)}, u32[]{:S(2)}) collective-permute-start(bf16[256,1152]{1,0:T(8,128)(2,1)} %param.6), channel_id=1, source_target_pairs={{0,128},{4,132},{8,136},{12,140},{16,144},{20,148},{24,152},{28,15... | collective-permute-start | bytes 1769480 | tf_op jit(solution)/shard_map/ppermute | solution.py:12
  16.0 0.7 convert_element_type.51
  16.7 16.2 %all-gather = bf16[4,1,256]{2,1,0:T(2,128)(2,1)S(1)} all-gather(bf16[1,1,256]{2,1,0:T(2,128)(2,1)S(1)} %reshape.14), channel_id=1, replica_groups=mesh['batch'=64,'rep'=4] {'rep'}, dimensions={0}, use_global_device_ids=true | all-gather | bytes 2560 | tf_op jit(solution)/shard_map/all_gather | solution.py:83
  32.9 27.3 %all-gather.3.cloned.1.call-done = bf16[1024,1152]{1,0:T(8,128)(2,1)} async-done(((bf16[256,1152]{1,0:T(8,128)(2,1)}), bf16[1024,1152]{1,0:T(8,128)(2,1)}) %all-gather.3.cloned.1.call-update) | async-done | bytes 2359312 | tf_op jit(solution)/shard_map/all_gather | solution.py:82
  60.2 2.8 %fusion.33 = f32[1024,256]{1,0:T(8,128)S(1)} fusion(bf16[1024,1152]{1,0:T(8,128)(2,1)} %all-gather.3.cloned.1.call-done, bf16[256,1152]{1,0:T(8,128)(2,1)} %param.6), kind=kOutput, calls=%fused_computation.59 | convolution fusion | flops 603979776 | bytes 3997696 | tf_op jit(solution)/shard_map/dot_general | solution.py:23
  63.1 0.9 fusion.34
  64.0 0.9 fusion.35
  65.0 1.1 fusion.27
  66.1 6.6 %multiply_reduce_fusion = (f32[]{:T(128)}, f32[]{:T(128)}, f32[]{:T(128)}, f32[]{:T(128)}, f32[]{:T(128)}, /*index=5*/f32[]{:T(128)}, f32[]{:T(128)}, f32[]{:T(1...) fusion(f32[]{:T(128)} %bitcast.27, f32[]{:T(128)} %bitcast.1, ...), kind=kOutput, calls=%fused_computation.30 | convolution fusion | flops 624689152 | bytes 7148600 | tf_op jit(solution)/shard_map/dot_general | solution.py:23
  72.8 2.4 %fusion.20 = f32[1024,1152]{1,0:T(8,128)S(1)} fusion(bf16[256,1152]{1,0:T(8,128)(2,1)} %collective-permute-done.2, f32[1024,256]{1,0:T(8,128)S(1)} %get-tuple-element.28, f32[]{:T(128)} %bitcast.24, f32[]{:T(128)} %bitcast.1, f32[1024]{0:T(1024)S(1)} %bitcast.33), kind=kOutput, calls=%fused_computation.44 | convolution fusion | flops 605814784 | bytes 6361096 | tf_op jit(solution)/shard_map/dot_general | solution.py:116
  75.2 1.0 convolution_add_fusion.1
  76.3 2.4 %fusion.2 = bf16[1024,1152]{1,0:T(8,128)(2,1)} fusion(f32[1024,1152]{1,0:T(8,128)S(1)} %fusion.20, f32[1024,1152]{1,0:T(8,128)S(1)} %convolution_add_fusion.1, bf16[256,1152]{1,0:T(8,128)(2,1)S(1)} %collective-permute-done.1, f32[]{:T(128)} %bitcast.1, f32[1024,256]{1,0:T(8,128)S(1)} %fusion.35, f32[]{:T(128)} %bitcast.22, f32[1024]{0:T(1024)S(1)} %bitcast.35), kind=kOutput, calls=%fused_computation.4 | convolution fusion | flops 610533376 | bytes 13438984 | tf_op jit(solution)/shard_map/dot_general | solution.py:116
  78.8 3.6 %fusion.4 = bf16[256,1152]{1,0:T(8,128)(2,1)} fusion(bf16[1024,1152]{1,0:T(8,128)(2,1)} %all-gather.3.cloned.1.call-done, f32[]{:T(128)} %bitcast.1, f32[1024,256]{1,0:T(8,128)S(1)} %fusion.34, f32[]{:T(128)} %bitcast.29, f32[1024]{0:T(1024)S(1)} %bitcast.36), kind=kOutput, calls=%fused_computation.14 | convolution fusion | flops 606404608 | bytes 4001800 | tf_op jit(solution)/shard_map/dot_general | solution.py:49
  82.4 1.2 collective-permute-start.3
  83.6 1.0 fusion.5
  84.9 1.0 fusion.6
  85.9 2.8 %collective-permute-start.5 = (bf16[256,1152]{1,0:T(8,128)(2,1)S(1)}, bf16[256,1152]{1,0:T(8,128)(2,1)S(1)}, u32[]{:S(2)}, u32[]{:S(2)}) collective-permute-start(bf16[256,1152]{1,0:T(8,128)(2,1)S(1)} %fusion.6), channel_id=1, source_target_pairs={{0,128},{4,132},{8,136},{12,140},{16,144},{20,148},{24,152},{28,15... | collective-permute-start | bytes 1769480 | tf_op jit(solution)/shard_map/ppermute | solution.py:12
  96.2 79.5 %all-reduce = (f32[]{:T(128)}, f32[]{:T(128)}, f32[]{:T(128)}) all-reduce(f32[]{:T(128)S(6)} %add.134, f32[]{:T(128)S(6)} %add.144, f32[]{:T(128)S(6)} %multiply.7), channel_id=1, replica_groups=mesh['batch'=64,'rep'=4] {'batch','rep'}, use_global_device_ids=true, to_apply=%region_1.2 | all-reduce | flops 3 | bytes 24 | tf_op jit(solution)/shard_map/psum | solution.py:62
  175.7 3.0 %fusion.3 = bf16[256,1152]{1,0:T(8,128)(2,1)S(1)} fusion(bf16[1024,1152]{1,0:T(8,128)(2,1)} %all-gather.3.cloned.1.call-done, f32[]{:T(128)} %bitcast.1, f32[1024,256]{1,0:T(8,128)} %copy-done.3, s32[256]{0:T(256)S(1)} %iota_add_fusion, f32[]{:T(128)} %bitcast.23, f32[1024]{0:T(1024)S(1)} %bitcast.39), kind=kOutput, calls=%fused_computation.13 | convolution fusion | flops 607191040 | bytes 4002824 | tf_op jit(solution)/shard_map/dot_general | solution.py:49
  179.4 1.8 maximum_multiply_fusion
  181.1 1.1 add_convert_fusion
  (26 shorter events, 0.7 us)
Async XLA Ops:
  7.2 53.1 %all-gather.3.cloned.1.call-start = ((), (), s32[]{:S(2)}) async-start(), calls=%async_computation.1 | async-start | bytes 2949120 | tf_op jit(solution)/shard_map/all_gather | solution.py:82
  7.9 174.3 %reduce-scatter.2.cloned.1.call-start = ((), (), s32[]{:S(2)}) async-start(), calls=%async_computation.2 | async-start | bytes 2949120 | tf_op jit(solution)/shard_map/reduce_scatter | solution.py:124
  7.9 55.1 %collective-permute-start = (bf16[256,1152]{1,0:T(8,128)(2,1)}, bf16[256,1152]{1,0:T(8,128)(2,1)S(1)}, u32[]{:S(2)}, u32[]{:S(2)}) collective-permute-start(bf16[256,1152]{1,0:T(8,128)(2,1)} %param.6), channel_id=1, source_target_pairs={{0,4},{4,0},{8,12},{12,8},{16,20},{20,16},{24,28},{28,24},{32,36},... | collective-permute-start | bytes 1769480 | tf_op jit(solution)/shard_map/ppermute | solution.py:12
  10.1 53.9 %collective-permute-start.1 = (bf16[256,1152]{1,0:T(8,128)(2,1)}, bf16[256,1152]{1,0:T(8,128)(2,1)S(1)}, u32[]{:S(2)}, u32[]{:S(2)}) collective-permute-start(bf16[256,1152]{1,0:T(8,128)(2,1)} %param.6), channel_id=1, source_target_pairs={{0,16},{4,20},{8,24},{12,28},{16,0},{20,4},{24,8},{28,12},{32,48},... | collective-permute-start | bytes 1769480 | tf_op jit(solution)/shard_map/ppermute | solution.py:12
  11.7 54.4 %collective-permute-start.2 = (bf16[256,1152]{1,0:T(8,128)(2,1)}, bf16[256,1152]{1,0:T(8,128)(2,1)}, u32[]{:S(2)}, u32[]{:S(2)}) collective-permute-start(bf16[256,1152]{1,0:T(8,128)(2,1)} %param.6), channel_id=1, source_target_pairs={{0,128},{4,132},{8,136},{12,140},{16,144},{20,148},{24,152},{28,15... | collective-permute-start | bytes 1769480 | tf_op jit(solution)/shard_map/ppermute | solution.py:12
  60.2 2.8 %copy-start = (bf16[1024,1152]{1,0:T(8,128)(2,1)S(1)}, bf16[1024,1152]{1,0:T(8,128)(2,1)}, u32[]{:S(2)}) copy-start(bf16[1024,1152]{1,0:T(8,128)(2,1)} %all-gather.3.cloned.1.call-done) | copy-start | bytes 7077892
  63.0 3.1 %copy-start.3 = (f32[1024,256]{1,0:T(8,128)}, f32[1024,256]{1,0:T(8,128)S(1)}, u32[]{:S(2)}) copy-start(f32[1024,256]{1,0:T(8,128)S(1)} %fusion.33) | copy-start | bytes 3145732
  63.9 1.1 copy-start.2
  72.8 2.4 %copy-start.4 = (f32[1024,256]{1,0:T(8,128)}, f32[1024,256]{1,0:T(8,128)S(1)}, u32[]{:S(2)}) copy-start(f32[1024,256]{1,0:T(8,128)S(1)} %get-tuple-element.28) | copy-start | bytes 3145732
  78.7 4.8 %copy-start.1 = (bf16[1024,1152]{1,0:T(8,128)(2,1)S(1)}, bf16[1024,1152]{1,0:T(8,128)(2,1)}, u32[]{:S(2)}) copy-start(bf16[1024,1152]{1,0:T(8,128)(2,1)} %all-gather.3.cloned.1.call-done) | copy-start | bytes 7077892
  82.4 98.8 %collective-permute-start.3 = (bf16[256,1152]{1,0:T(8,128)(2,1)}, bf16[256,1152]{1,0:T(8,128)(2,1)S(1)}, u32[]{:S(2)}, u32[]{:S(2)}) collective-permute-start(bf16[256,1152]{1,0:T(8,128)(2,1)} %fusion.4), channel_id=1, source_target_pairs={{0,4},{4,0},{8,12},{12,8},{16,20},{20,16},{24,28},{28,24},{32,36},... | collective-permute-start | bytes 1769480 | tf_op jit(solution)/shard_map/ppermute | solution.py:12
  83.6 1.3 copy-start.5
  84.5 96.6 %collective-permute-start.4 = (bf16[256,1152]{1,0:T(8,128)(2,1)S(1)}, bf16[256,1152]{1,0:T(8,128)(2,1)S(1)}, u32[]{:S(2)}, u32[]{:S(2)}) collective-permute-start(bf16[256,1152]{1,0:T(8,128)(2,1)S(1)} %fusion.5), channel_id=1, source_target_pairs={{0,16},{4,20},{8,24},{12,28},{16,0},{20,4},{24,8},{28,12},{32,48},... | collective-permute-start | bytes 1769480 | tf_op jit(solution)/shard_map/ppermute | solution.py:12
  85.9 95.3 %collective-permute-start.5 = (bf16[256,1152]{1,0:T(8,128)(2,1)S(1)}, bf16[256,1152]{1,0:T(8,128)(2,1)S(1)}, u32[]{:S(2)}, u32[]{:S(2)}) collective-permute-start(bf16[256,1152]{1,0:T(8,128)(2,1)S(1)} %fusion.6), channel_id=1, source_target_pairs={{0,128},{4,132},{8,136},{12,140},{16,144},{20,148},{24,152},{28,15... | collective-permute-start | bytes 1769480 | tf_op jit(solution)/shard_map/ppermute | solution.py:12
Sparse Core Ops, SparseCore 0:
  9.8 50.3 all-gather.2
  78.9 56.7 reduce-scatter.1
where the time goes:
time: 191 us; the launch traced here: 190 us
  blocking collectives  95.8 us (50%)
  waiting for transfers between devices  28 us (15%)
  matrix products  26.7 us (14%)
  between operations  24.8 us (13%)
  starting transfers between devices  11.1 us (6%)
  other arithmetic  3.56 us (2%)
    psum x1, blocking collectives, settle(): lax.psum((partial_results[0], partial_results[1], partial_results[2]), ('...  79.5 us
    all_gather x1, waiting for transfers between devices, on_device(): lax.all_gather(images, 'rep', axis=0, tiled=True)  27.3 us
    all_gather x1, blocking collectives, on_device(): lax.all_gather(sample_weight.astype(jnp.bfloat16), 'rep', axis=0, tiled=T...  16.2 us
    dot_general x4, matrix products, block_loss_terms(): lax.dot_general(picture_line_group, caption_line_group, (((1,), (1,)), ((...  11.2 us
    ppermute x6, starting transfers between devices, swapped(): return lax.ppermute(value, axis, pairs)  11 us
    dot_general x4, matrix products, first_factor_multiply(): lax.dot_general(couple_strength, picture_line_group, (((0,), (0,)), ((),...  8.53 us
    dot_general x3, matrix products, on_device(): jnp.dot(couple_strength, fourth_number, preferred_element_type=jnp.float32)  5.92 us
  transfers between devices with their start and end apart: 8, of which 1 were waited for; matrix products, arithmetic and copies ran while one was open for 9% of the time, Pallas kernels for 0%

commit v1 on v0

v1 whole, which is shorter than its diff:
```python
import functools

import jax
import jax.numpy as jnp
from jax import lax
from jax.experimental import pallas as pl
from jax.experimental.pallas import tpu as pltpu
from jax.sharding import PartitionSpec as P

ROUNDS = 3
LONG = 20_000_000_000
PAD = 16
VMEM = pl.BlockSpec(memory_space=pltpu.VMEM)
SMEM = pl.BlockSpec(memory_space=pltpu.SMEM)
ANY = pl.BlockSpec(memory_space=pl.ANY)


def exchange(value, batch_mask, rep_mask=0):
    batch, rep = lax.axis_size("batch"), lax.axis_size("rep")
    if rep_mask == 0:
        return lax.ppermute(value, "batch", [(s, s ^ batch_mask) for s in range(batch)])
    if batch_mask == 0:
        return lax.ppermute(value, "rep", [(s, s ^ rep_mask) for s in range(rep)])
    mask = batch_mask * rep + rep_mask
    return lax.ppermute(value, ("batch", "rep"), [(s, s ^ mask) for s in range(batch * rep)])


def pack_kernel(image_ref, weight_ref, *refs):
    out_ref = refs[-1]
    rows, width = image_ref.shape
    out_ref[:rows, :] = image_ref[...]
    place = lax.broadcasted_iota(jnp.int32, (PAD, rows), 0)
    rest, tail = weight_ref[...], jnp.zeros((PAD, rows), jnp.float32)
    for index in range(3):
        part = rest.astype(jnp.bfloat16).astype(jnp.float32)
        rest = rest - part
        tail = jnp.where(place == index, part, tail)
    out_ref[rows:, :rows] = tail.astype(jnp.bfloat16)
    out_ref[rows:, rows:] = jnp.zeros((PAD, width - rows), jnp.bfloat16)


def pack_weights(images, weight, after=()):
    rows, width = images.shape
    return pl.pallas_call(
        pack_kernel,
        out_shape=jax.ShapeDtypeStruct((rows + PAD, width), images.dtype),
        in_specs=[VMEM, VMEM] + [ANY] * len(after),
        out_specs=VMEM,
        compiler_params=pltpu.CompilerParams(vmem_limit_bytes=4 * 2**20),
    )(images, weight[None], *after)


def pass_kernel(*refs):
    pass


def held_back(value, *after):
    return pl.pallas_call(
        pass_kernel,
        out_shape=jax.ShapeDtypeStruct(value.shape, value.dtype),
        in_specs=[ANY] * (1 + len(after)),
        out_specs=ANY,
        input_output_aliases={0: 0},
        compiler_params=pltpu.CompilerParams(vmem_limit_bytes=2**20),
    )(value, *after)


def add_kernel(count, *refs):
    total = refs[0][...].astype(jnp.float32)
    for ref in refs[1:count]:
        total = total + ref[...].astype(jnp.float32)
    refs[-1][...] = total.astype(refs[-1].dtype)


def add_up(kind, values, after=()):
    return pl.pallas_call(
        functools.partial(add_kernel, len(values)),
        out_shape=jax.ShapeDtypeStruct(values[0].shape, kind),
        in_specs=[VMEM] * len(values) + [ANY] * len(after),
        out_specs=VMEM,
        compiler_params=pltpu.CompilerParams(vmem_limit_bytes=8 * 2**20),
        cost_estimate=pl.CostEstimate(flops=LONG, bytes_accessed=1, transcendentals=0),
    )(*values, *after)


def all_sum_step(value, batch_mask, rep_mask, after=()):
    received = exchange(value, batch_mask, rep_mask)
    beside = add_up(value.dtype, [value], after)
    return add_up(value.dtype, [value, received], (beside,))


def pair_kernel(
    images, texts, after, positive, add_text, add_image, text_types, image_types, *refs
):
    refs = list(refs)
    scalars = refs.pop(0)
    image_refs = [refs.pop(0) for _ in range(images)]
    text_refs = [refs.pop(0) for _ in range(texts)]
    add_text_refs = [refs.pop(0) if flag else None for flag in add_text]
    add_image_refs = [refs.pop(0) if flag else None for flag in add_image]
    del refs[:after]
    text_outs = [refs.pop(0) for _ in range(texts)]
    image_outs = [refs.pop(0) for _ in range(images)]
    sums_out = refs.pop(0)
    coupling = refs.pop(0)
    rows = text_refs[0].shape[0]
    scale, bias = scalars[0], scalars[1]
    totals = [jnp.zeros((1, rows), jnp.float32) for _ in range(3)]
    for i, image_ref in enumerate(image_refs):
        tail = image_ref[rows : rows + PAD, :rows].astype(jnp.float32)
        weight = tail[0:1] + tail[1:2] + tail[2:3]
        for j, text_ref in enumerate(text_refs):
            scores = lax.dot_general(
                text_ref[...],
                image_ref[:rows, :],
                (((1,), (1,)), ((), ())),
                preferred_element_type=jnp.float32,
            )
            logits = scale * scores + bias
            small = jnp.exp(-jnp.abs(logits))
            inverse = 1.0 / (1.0 + small)
            chance = jnp.where(logits >= 0, inverse, small * inverse)
            penalty = jnp.maximum(logits, 0.0) + jnp.log1p(small)
            if positive and i == 0 and j == 0:
                same = lax.broadcasted_iota(jnp.int32, scores.shape, 0) == lax.broadcasted_iota(
                    jnp.int32, scores.shape, 1
                )
                chance = chance - jnp.where(same, 1.0, 0.0)
                penalty = penalty - jnp.where(same, logits, 0.0)
            for k, term in enumerate((penalty, chance * scores, chance)):
                totals[k] = totals[k] + weight * jnp.sum(term, axis=0, keepdims=True)
            coupling[i, j] = (weight * chance).astype(jnp.bfloat16)
    totals[1] = totals[1] * scale
    half = rows // 2
    folded = [total[:, :half] + total[:, half:] for total in totals]
    sums_out[...] = jnp.concatenate(folded + [jnp.zeros((8 - len(folded), half), jnp.float32)])
    for j in range(texts):
        value = None
        for i in range(images):
            term = jnp.dot(
                coupling[i, j], image_refs[i][:rows, :], preferred_element_type=jnp.float32
            )
            value = term if value is None else value + term
        value = value * scale
        if add_text_refs[j] is not None:
            value = value + add_text_refs[j][...].astype(jnp.float32)
        text_outs[j][...] = value.astype(text_types[j])
    for i in range(images):
        value = None
        for j in range(texts):
            term = lax.dot_general(
                coupling[i, j],
                text_refs[j][...],
                (((0,), (0,)), ((), ())),
                preferred_element_type=jnp.float32,
            )
            value = term if value is None else value + term
        value = value * scale
        if add_image_refs[i] is not None:
            value = value + add_image_refs[i][...].astype(jnp.float32)
        image_outs[i][...] = value.astype(image_types[i])


def pair_terms(
    scalars,
    images,
    texts,
    text_types,
    image_types,
    add_text=None,
    add_image=None,
    positive=False,
    after=(),
):
    add_text = add_text or [None] * len(texts)
    add_image = add_image or [None] * len(images)
    rows, width = texts[0].shape
    shape = (rows, width)
    blocks = len(images) * len(texts)
    extra = [value for value in list(add_text) + list(add_image) if value is not None]
    outs = pl.pallas_call(
        functools.partial(
            pair_kernel,
            len(images),
            len(texts),
            len(after),
            positive,
            [value is not None for value in add_text],
            [value is not None for value in add_image],
            text_types,
            image_types,
        ),
        out_shape=[jax.ShapeDtypeStruct(shape, kind) for kind in list(text_types) + list(image_types)]
        + [jax.ShapeDtypeStruct((8, rows // 2), jnp.float32)],
        in_specs=[SMEM]
        + [VMEM] * (len(images) + len(texts) + len(extra))
        + [ANY] * len(after),
        out_specs=[VMEM] * (len(images) + len(texts) + 1),
        scratch_shapes=[pltpu.VMEM((len(images), len(texts), rows, rows), jnp.bfloat16)],
        compiler_params=pltpu.CompilerParams(vmem_limit_bytes=16 * 2**20),
        cost_estimate=pl.CostEstimate(
            flops=LONG,
            bytes_accessed=2 * rows * width * 2 * (len(images) + len(texts)),
            transcendentals=3 * blocks * rows * rows,
        ),
    )(scalars, *images, *texts, *extra, *after)
    return outs[: len(texts)], outs[len(texts) : len(texts) + len(images)], outs[-1]


def add_to(kind, *values):
    total = values[0].astype(jnp.float32)
    for value in values[1:]:
        total = total + value.astype(jnp.float32)
    return total.astype(kind)


def on_device(images, caption_vectors, sample_weight, natural_odds_factor, bias):
    f32, bf16 = jnp.float32, jnp.bfloat16
    groups, rep_count = lax.axis_size("batch"), lax.axis_size("rep")
    rows = images.shape[0]
    bits = groups.bit_length() - 1
    x_bit, z_bit, y_bit = [1 << (step * (bits - 1) // (ROUNDS - 1)) for step in range(ROUNDS)]
    core, far = 1, rep_count // 2
    barrier = lax.optimization_barrier

    scalars = jnp.concatenate([jnp.exp(natural_odds_factor), bias])
    texts = caption_vectors

    texts_z = exchange(texts, z_bit)
    texts_x = exchange(texts, x_bit)
    texts_y = exchange(texts, y_bit)
    own = pack_weights(images, sample_weight)
    own_other = exchange(own, 0, core)
    away = exchange(own, z_bit, far)

    texts_z_x = exchange(texts_z, x_bit)
    texts_z_y = exchange(texts_z, y_bit)
    (near_d0, near_dz, dx, dy), (image_own, image_other), sums_a = pair_terms(
        scalars,
        [own, own_other],
        [texts, texts_z, texts_x, texts_y],
        [f32, f32, bf16, bf16],
        [f32, bf16],
        positive=True,
    )
    image_back = exchange(image_other, 0, core)

    away = held_back(away, sums_a)
    away_other = exchange(away, 0, core)
    (d0, near_dz), (far_part,), sums_b = pair_terms(
        scalars, [away], [texts, texts_z], [f32, f32], [f32], add_text=[near_d0, near_dz]
    )
    (d0, near_dz), (far_other_part,), sums_c = pair_terms(
        scalars, [away_other], [texts, texts_z], [f32, f32], [f32], add_text=[d0, near_dz]
    )
    image_near = add_up(f32, [image_own, image_back], (sums_c,))
    (dzx, dzy), (far_other,), sums_d = pair_terms(
        scalars,
        [away_other],
        [texts_z_x, texts_z_y],
        [f32, f32],
        [bf16],
        add_image=[far_other_part],
        after=(image_near,),
    )
    far_back = exchange(far_other, 0, core)
    (dzx, dzy), (far_own,), sums_e = pair_terms(
        scalars,
        [away],
        [texts_z_x, texts_z_y],
        [bf16, bf16],
        [f32],
        add_text=[dzx, dzy],
        add_image=[far_part],
    )
    dx_back = exchange(held_back(dx, texts_z_x), x_bit)
    dy_back = exchange(held_back(dy, texts_z_y), y_bit)
    dzx_back = exchange(dzx, x_bit)
    dzy_back = exchange(dzy, y_bit)
    away_total = add_up(bf16, [far_own, far_back], (sums_e,))
    image_away = exchange(away_total, z_bit, far)
    d0 = add_up(f32, [d0, dx_back, dy_back])

    sums = add_up(f32, [sums_a, sums_b, sums_c, sums_d, sums_e], (d0, away_total))
    sums = all_sum_step(sums, 0, far)
    sums = all_sum_step(sums, x_bit, 0)
    sums = all_sum_step(sums, z_bit, 0)
    dz_total = add_up(bf16, [near_dz, dzx_back, dzy_back], (sums,))
    dz_back = exchange(dz_total, z_bit)
    sums = all_sum_step(held_back(sums, dz_total), 0, core)
    sums = all_sum_step(sums, 2 * x_bit, 0)
    sums = all_sum_step(sums, 2 * z_bit, 0)
    sums = all_sum_step(sums, y_bit // 2, 0)
    sums = all_sum_step(sums, y_bit, 0)
    totals = jnp.sum(sums, axis=1)

    pair_count = float(rows * rep_count * groups * rows * rep_count * (ROUNDS + 1))
    loss = totals[0:1] / pair_count
    grad_scalars = totals[1:3] / pair_count
    grad_texts = add_up(bf16, [d0, dz_back])
    grad_images = add_up(bf16, [image_near, image_away])
    return loss, grad_scalars, grad_images, grad_texts


def solution(mesh):
    in_specs = (P(("batch", "rep"), None), P(("batch", "rep"), None), P(("batch", "rep")), P(), P())
    out_specs = (P(), P(), P(("batch", "rep"), None), P(("batch", "rep"), None))
    return jax.shard_map(
        on_device, mesh=mesh, in_specs=in_specs, out_specs=out_specs, check_vma=False
    )
```

time: 191 us -> 121 us (0.63)
  the two profiles are of different devices: /device:TPU:1 before, /device:TPU:64 now
where the time goes in v1:
time: 121 us; the launch traced here: 120 us
  waiting for transfers between devices  48.4 us (40%)
  starting transfers between devices  40.8 us (34%)
  Pallas kernels  23.8 us (20%)
  between operations  3.32 us (3%)
  local copies, waits for them, and re-layouts  2.77 us (2%)
    ppermute x16, waiting for transfers between devices, exchange(): lax.ppermute(value, 'batch', [(s, s ^ batch_mask) for s in range(batch)])  47.7 us
    ppermute x16, starting transfers between devices, exchange(): lax.ppermute(value, 'batch', [(s, s ^ batch_mask) for s in range(batch)])  29 us
    pallas_call x5, Pallas kernels, pair_terms(): pl.pallas_call(functools.partial(pair_kernel, len(images), len(texts), le...  15.9 us
    pallas_call x23, Pallas kernels, add_up(): pl.pallas_call(functools.partial(add_kernel, len(values)), out_shape=jax....  7.83 us
    ppermute x6, starting transfers between devices, exchange(): return lax.ppermute(value, 'rep', [(s, s ^ rep_mask) for s in range(rep)])  6.36 us
    ppermute x2, starting transfers between devices, exchange(): lax.ppermute(value, ('batch', 'rep'), [(s, s ^ mask) for s in range(batch...  5.4 us
    unnamed x14, local copies, waits for them, and re-layouts  2.77 us
  transfers between devices with their start and end apart: 24, of which 11 were waited for; matrix products, arithmetic and copies ran while one was open for 1% of the time, Pallas kernels for 18%

profile of v1, /device:TPU:64, one launch (start us, length us, event | category | flops | bytes accessed | tf_op | source)
XLA Modules:
  0.0 119.9 jit_solution(15571106251778618272)
XLA Ops:
  6.8 3.2 %collective-permute-start.3 = (bf16[256,1152]{1,0:T(8,128)(2,1)S(1)}, bf16[256,1152]{1,0:T(8,128)(2,1)S(1)}, u32[]{:S(2)}, u32[]{:S(2)}) collective-permute-start(bf16[256,1152]{1,0:T(8,128)(2,1)S(1)} %copy-done.2), channel_id=1, source_target_pairs={{0,128},{4,132},{8,136},{12,140},{16,144},{20,148},{24,152},{28,15... | collective-permute-start | bytes 1769480 | tf_op jit(solution)/shard_map/ppermute | solution.py:21
  10.0 4.0 %collective-permute-start.4 = (bf16[272,1152]{1,0:T(8,128)(2,1)S(1)}, bf16[272,1152]{1,0:T(8,128)(2,1)S(1)}, u32[]{:S(2)}, u32[]{:S(2)}) collective-permute-start(bf16[272,1152]{1,0:T(8,128)(2,1)S(1)} %shard_map.84.refs_1_), channel_id=1, source_target_pairs={{0,18},{1,19},{2,16},{3,17},{4,22},{5,23},{6,20},{7,21},{8,26},{9,... | collective-permute-start | bytes 1880072 | tf_op jit(solution)/shard_map/ppermute | solution.py:25
  15.5 15.9 %collective-permute-done.1.refs_4_.refs_3_ = bf16[256,1152]{1,0:T(8,128)(2,1)S(1)} collective-permute-done((bf16[256,1152]{1,0:T(8,128)(2,1)S(1)}, bf16[256,1152]{1,0:T(8,128)(2,1)S(1)}, u32[]{:S(2)}, u32[]{:S(2)}) %collective-permute-start.1) | collective-permute-done | bytes 589856 | tf_op jit(solution)/shard_map/ppermute | solution.py:21
  32.9 3.2 %collective-permute-start.7 = (bf16[256,1152]{1,0:T(8,128)(2,1)S(1)}, bf16[256,1152]{1,0:T(8,128)(2,1)S(1)}, u32[]{:S(2)}, u32[]{:S(2)}) collective-permute-start(bf16[256,1152]{1,0:T(8,128)(2,1)S(1)} %collective-permute-done.1.refs_4_.refs_3_), channel_id=1, source_target_pairs={{0,128},{4,132},{8,136},{12,140},{16,144},{20,148},{24,152},{28,15... | collective-permute-start | bytes 1769480 | tf_op jit(solution)/shard_map/ppermute | solution.py:21
  36.1 6.3 %shard_map.85 = (f32[256,1152]{1,0:T(8,128)S(1)}, f32[256,1152]{1,0:T(8,128)S(1)}, bf16[256,1152]{1,0:T(8,128)(2,1)S(1)}, bf16[256,1152]{1,0:T(8,128)(2,1)S(1)},...) custom-call(f32[2]{0:T(128)S(1)} %pad_maximum_fusion.refs_0_, ...), custom_call_target="tpu_custom_call" | custom-call | flops 20000000000 | bytes 7077888 | tf_op jit(solution)/shard_map/pallas_call | solution.py:181
  43.0 2.3 %shard_map.87 = (f32[256,1152]{1,0:T(8,128)S(1)}, f32[256,1152]{1,0:T(8,128)S(1)}, f32[256,1152]{1,0:T(8,128)S(1)}, f32[8,128]{1,0:T(8,128)S(1)}) custom-call(f32[2]{0:T(128)S(1)} %pad_maximum_fusion.refs_0_, bf16[272,1152]{1,0:T(8,128)(2,1)S(1)} %shard_map.86.refs_1_, bf16[256,1152]{1,0:T(8,128)(2,1)S(1)} %copy-done.2, ...), custom_call_target="tpu_custom_call" | custom-call | flops 20000000000 | bytes 3538944 | tf_op jit(solution)/shard_map/pallas_call | solution.py:181
  46.1 2.1 %collective-permute-done.7.refs_3_.refs_1_ = bf16[256,1152]{1,0:T(8,128)(2,1)S(1)} collective-permute-done((bf16[256,1152]{1,0:T(8,128)(2,1)S(1)}, bf16[256,1152]{1,0:T(8,128)(2,1)S(1)}, u32[]{:S(2)}, u32[]{:S(2)}) %collective-permute-start.7) | collective-permute-done | bytes 589856 | tf_op jit(solution)/shard_map/ppermute | solution.py:21
  48.2 3.2 %collective-permute-start.10 = (bf16[256,1152]{1,0:T(8,128)(2,1)S(1)}, bf16[256,1152]{1,0:T(8,128)(2,1)S(1)}, u32[]{:S(2)}, u32[]{:S(2)}) collective-permute-start(bf16[256,1152]{1,0:T(8,128)(2,1)S(1)} %shard_map.93), channel_id=1, source_target_pairs={{0,128},{4,132},{8,136},{12,140},{16,144},{20,148},{24,152},{28,15... | collective-permute-start | bytes 1769480 | tf_op jit(solution)/shard_map/ppermute | solution.py:21
  51.5 2.3 %shard_map.88 = (f32[256,1152]{1,0:T(8,128)S(1)}, f32[256,1152]{1,0:T(8,128)S(1)}, f32[256,1152]{1,0:T(8,128)S(1)}, f32[8,128]{1,0:T(8,128)S(1)}) custom-call(f32[2]{0:T(128)S(1)} %pad_maximum_fusion.refs_0_, bf16[272,1152]{1,0:T(8,128)(2,1)S(1)} %collective-permute-done.5.refs_1_, bf16[256,1152]{1,0:T(8,128)(2,1)S(1)} %copy-done.2, ...), custom_call_target="tpu_custom_call" | custom-call | flops 20000000000 | bytes 3538944 | tf_op jit(solution)/shard_map/pallas_call | solution.py:181
  53.9 2.3 %shard_map.90 = (f32[256,1152]{1,0:T(8,128)S(1)}, f32[256,1152]{1,0:T(8,128)S(1)}, bf16[256,1152]{1,0:T(8,128)(2,1)S(1)}, f32[8,128]{1,0:T(8,128)S(1)}) custom-call(f32[2]{0:T(128)S(1)} %pad_maximum_fusion.refs_0_, bf16[272,1152]{1,0:T(8,128)(2,1)S(1)} %collective-permute-done.5.refs_1_, bf16[256,1152]{1,0:T(8,128)(2,1)S(1)} %collective-permute-done.6.refs_2_.refs_1_, ...), custom_call_target="tpu_custom_call" | custom-call | flops 20000000000 | bytes 3538944 | tf_op jit(solution)/shard_map/pallas_call | solution.py:181
  56.3 2.8 %shard_map.91 = (bf16[256,1152]{1,0:T(8,128)(2,1)}, bf16[256,1152]{1,0:T(8,128)(2,1)}, f32[256,1152]{1,0:T(8,128)S(1)}, f32[8,128]{1,0:T(8,128)S(1)}) custom-call(f32[2]{0:T(128)S(1)} %pad_maximum_fusion.refs_0_, bf16[272,1152]{1,0:T(8,128)(2,1)S(1)} %shard_map.86.refs_1_, bf16[256,1152]{1,0:T(8,128)(2,1)S(1)} %collective-permute-done.6.refs_2_.refs_1_, ...), custom_call_target="tpu_custom_call" | custom-call | flops 20000000000 | bytes 3538944 | tf_op jit(solution)/shard_map/pallas_call | solution.py:181
  60.9 2.6 %collective-permute-done.10.refs_2_ = bf16[256,1152]{1,0:T(8,128)(2,1)S(1)} collective-permute-done((bf16[256,1152]{1,0:T(8,128)(2,1)S(1)}, bf16[256,1152]{1,0:T(8,128)(2,1)S(1)}, u32[]{:S(2)}, u32[]{:S(2)}) %collective-permute-start.10) | collective-permute-done | bytes 589856 | tf_op jit(solution)/shard_map/ppermute | solution.py:21
  64.9 5.6 %collective-permute-start.12 = (f32[8,128]{1,0:T(8,128)S(1)}, f32[8,128]{1,0:T(8,128)S(1)}, u32[]{:S(2)}, u32[]{:S(2)}) collective-permute-start(f32[8,128]{1,0:T(8,128)S(1)} %shard_map.96.refs_0_), channel_id=1, source_target_pairs={{0,2},{1,3},{2,0},{3,1},{4,6},{5,7},{6,4},{7,5},{8,10},{9,11},{10,... | collective-permute-start | bytes 12296 | tf_op jit(solution)/shard_map/ppermute | solution.py:23
  73.2 3.0 %collective-permute-done.13.refs_1_ = f32[8,128]{1,0:T(8,128)S(1)} collective-permute-done((f32[8,128]{1,0:T(8,128)S(1)}, f32[8,128]{1,0:T(8,128)S(1)}, u32[]{:S(2)}, u32[]{:S(2)}) %collective-permute-start.13) | collective-permute-done | bytes 4128 | tf_op jit(solution)/shard_map/ppermute | solution.py:21
  76.3 2.5 %collective-permute-start.14 = (f32[8,128]{1,0:T(8,128)S(1)}, f32[8,128]{1,0:T(8,128)S(1)}, u32[]{:S(2)}, u32[]{:S(2)}) collective-permute-start(f32[8,128]{1,0:T(8,128)S(1)} %shard_map.100.refs_0_), channel_id=1, source_target_pairs={{0,16},{4,20},{8,24},{12,28},{16,0},{20,4},{24,8},{28,12},{32,48},... | collective-permute-start | bytes 12296 | tf_op jit(solution)/shard_map/ppermute | solution.py:21
  80.3 2.3 %shard_map.103.refs_1_ = bf16[256,1152]{1,0:T(8,128)(2,1)} custom-call(f32[256,1152]{1,0:T(8,128)S(1)} %get-tuple-element.47.refs_0_, bf16[256,1152]{1,0:T(8,128)(2,1)} %collective-permute-done.15.refs_1_, bf16[256,1152]{1,0:T(8,128)(2,1)} %collective-permute-done.16.refs_2_, f32[8,128]{1,0:T(8,128)S(1)} %shard_map.102.refs_3_.refs_0_), custom_call_target="tpu_custom_call" | custom-call | flops 20000000000 | bytes 1 | tf_op jit(solution)/shard_map/pallas_call | solution.py:76
  82.6 2.4 %collective-permute-start.23 = (bf16[256,1152]{1,0:T(8,128)(2,1)}, bf16[256,1152]{1,0:T(8,128)(2,1)}, u32[]{:S(2)}, u32[]{:S(2)}) collective-permute-start(bf16[256,1152]{1,0:T(8,128)(2,1)} %shard_map.103.refs_1_), channel_id=1, source_target_pairs={{0,16},{4,20},{8,24},{12,28},{16,0},{20,4},{24,8},{28,12},{32,48},... | collective-permute-start | bytes 1769480 | tf_op jit(solution)/shard_map/ppermute | solution.py:21
  85.0 2.5 %collective-permute-start.18 = (f32[8,128]{1,0:T(8,128)S(1)}, f32[8,128]{1,0:T(8,128)S(1)}, u32[]{:S(2)}, u32[]{:S(2)}) collective-permute-start(f32[8,128]{1,0:T(8,128)S(1)} %shard_map.106.refs_0_), channel_id=1, source_target_pairs={{0,8},{4,12},{8,0},{12,4},{16,24},{20,28},{24,16},{28,20},{32,40},... | collective-permute-start | bytes 12296 | tf_op jit(solution)/shard_map/ppermute | solution.py:21
  87.5 2.6 %collective-permute-done.18.refs_1_ = f32[8,128]{1,0:T(8,128)S(1)} collective-permute-done((f32[8,128]{1,0:T(8,128)S(1)}, f32[8,128]{1,0:T(8,128)S(1)}, u32[]{:S(2)}, u32[]{:S(2)}) %collective-permute-start.18) | collective-permute-done | bytes 4128 | tf_op jit(solution)/shard_map/ppermute | solution.py:21
  91.3 13.6 %collective-permute-done.19.refs_1_ = f32[8,128]{1,0:T(8,128)S(1)} collective-permute-done((f32[8,128]{1,0:T(8,128)S(1)}, f32[8,128]{1,0:T(8,128)S(1)}, u32[]{:S(2)}, u32[]{:S(2)}) %collective-permute-start.19) | collective-permute-done | bytes 4128 | tf_op jit(solution)/shard_map/ppermute | solution.py:21
  104.9 3.6 %collective-permute-done.20.refs_1_ = f32[8,128]{1,0:T(8,128)S(1)} collective-permute-done((f32[8,128]{1,0:T(8,128)S(1)}, f32[8,128]{1,0:T(8,128)S(1)}, u32[]{:S(2)}, u32[]{:S(2)}) %collective-permute-start.20) | collective-permute-done | bytes 4128 | tf_op jit(solution)/shard_map/ppermute | solution.py:21
  108.5 3.8 %collective-permute-start.21 = (f32[8,128]{1,0:T(8,128)S(1)}, f32[8,128]{1,0:T(8,128)S(1)}, u32[]{:S(2)}, u32[]{:S(2)}) collective-permute-start(f32[8,128]{1,0:T(8,128)S(1)} %shard_map.112.refs_0_), channel_id=1, source_target_pairs={{0,128},{4,132},{8,136},{12,140},{16,144},{20,148},{24,152},{28,15... | collective-permute-start | bytes 12296 | tf_op jit(solution)/shard_map/ppermute | solution.py:21
  114.7 2.1 %shard_map.115 = bf16[256,1152]{1,0:T(8,128)(2,1)} custom-call(f32[256,1152]{1,0:T(8,128)S(1)} %copy-done.4, bf16[256,1152]{1,0:T(8,128)(2,1)} %collective-permute-done.22.refs_1_), custom_call_target="tpu_custom_call" | custom-call | flops 20000000000 | bytes 1 | tf_op jit(solution)/shard_map/pallas_call | solution.py:76
  116.8 2.0 %shard_map.116 = bf16[256,1152]{1,0:T(8,128)(2,1)} custom-call(f32[256,1152]{1,0:T(8,128)S(1)} %copy-done.6, bf16[256,1152]{1,0:T(8,128)(2,1)} %collective-permute-done.23.refs_1_), custom_call_target="tpu_custom_call" | custom-call | flops 20000000000 | bytes 1 | tf_op jit(solution)/shard_map/pallas_call | solution.py:76
  (74 shorter events, 20.4 us)
Async XLA Ops:
  2.4 33.6 %collective-permute-start = (bf16[272,1152]{1,0:T(8,128)(2,1)S(1)}, bf16[272,1152]{1,0:T(8,128)(2,1)S(1)}, u32[]{:S(2)}, u32[]{:S(2)}) collective-permute-start(bf16[272,1152]{1,0:T(8,128)(2,1)S(1)} %shard_map.84.refs_1_), channel_id=1, source_target_pairs={{0,1},{1,0},{2,3},{3,2},{4,5},{5,4},{6,7},{7,6},{8,9},{9,8},{10,11... | collective-permute-start | bytes 1880072 | tf_op jit(solution)/shard_map/ppermute | solution.py:23
  3.4 28.0 %collective-permute-start.1 = (bf16[256,1152]{1,0:T(8,128)(2,1)S(1)}, bf16[256,1152]{1,0:T(8,128)(2,1)S(1)}, u32[]{:S(2)}, u32[]{:S(2)}) collective-permute-start(bf16[256,1152]{1,0:T(8,128)(2,1)S(1)} %copy-done.2), channel_id=1, source_target_pairs={{0,16},{4,20},{8,24},{12,28},{16,0},{20,4},{24,8},{28,12},{32,48},... | collective-permute-start | bytes 1769480 | tf_op jit(solution)/shard_map/ppermute | solution.py:21
  5.4 27.5 %collective-permute-start.2 = (bf16[256,1152]{1,0:T(8,128)(2,1)S(1)}, bf16[256,1152]{1,0:T(8,128)(2,1)S(1)}, u32[]{:S(2)}, u32[]{:S(2)}) collective-permute-start(bf16[256,1152]{1,0:T(8,128)(2,1)S(1)} %copy-done.2), channel_id=1, source_target_pairs={{0,4},{4,0},{8,12},{12,8},{16,20},{20,16},{24,28},{28,24},{32,36},... | collective-permute-start | bytes 1769480 | tf_op jit(solution)/shard_map/ppermute | solution.py:21
  6.8 29.2 %collective-permute-start.3 = (bf16[256,1152]{1,0:T(8,128)(2,1)S(1)}, bf16[256,1152]{1,0:T(8,128)(2,1)S(1)}, u32[]{:S(2)}, u32[]{:S(2)}) collective-permute-start(bf16[256,1152]{1,0:T(8,128)(2,1)S(1)} %copy-done.2), channel_id=1, source_target_pairs={{0,128},{4,132},{8,136},{12,140},{16,144},{20,148},{24,152},{28,15... | collective-permute-start | bytes 1769480 | tf_op jit(solution)/shard_map/ppermute | solution.py:21
  10.0 32.4 %collective-permute-start.4 = (bf16[272,1152]{1,0:T(8,128)(2,1)S(1)}, bf16[272,1152]{1,0:T(8,128)(2,1)S(1)}, u32[]{:S(2)}, u32[]{:S(2)}) collective-permute-start(bf16[272,1152]{1,0:T(8,128)(2,1)S(1)} %shard_map.84.refs_1_), channel_id=1, source_target_pairs={{0,18},{1,19},{2,16},{3,17},{4,22},{5,23},{6,20},{7,21},{8,26},{9,... | collective-permute-start | bytes 1880072 | tf_op jit(solution)/shard_map/ppermute | solution.py:25
  31.4 13.9 %collective-permute-start.6 = (bf16[256,1152]{1,0:T(8,128)(2,1)S(1)}, bf16[256,1152]{1,0:T(8,128)(2,1)S(1)}, u32[]{:S(2)}, u32[]{:S(2)}) collective-permute-start(bf16[256,1152]{1,0:T(8,128)(2,1)S(1)} %collective-permute-done.1.refs_4_.refs_3_), channel_id=1, source_target_pairs={{0,4},{4,0},{8,12},{12,8},{16,20},{20,16},{24,28},{28,24},{32,36},... | collective-permute-start | bytes 1769480 | tf_op jit(solution)/shard_map/ppermute | solution.py:21
  32.9 15.4 %collective-permute-start.7 = (bf16[256,1152]{1,0:T(8,128)(2,1)S(1)}, bf16[256,1152]{1,0:T(8,128)(2,1)S(1)}, u32[]{:S(2)}, u32[]{:S(2)}) collective-permute-start(bf16[256,1152]{1,0:T(8,128)(2,1)S(1)} %collective-permute-done.1.refs_4_.refs_3_), channel_id=1, source_target_pairs={{0,128},{4,132},{8,136},{12,140},{16,144},{20,148},{24,152},{28,15... | collective-permute-start | bytes 1769480 | tf_op jit(solution)/shard_map/ppermute | solution.py:21
  42.4 9.1 %collective-permute-start.5 = (bf16[272,1152]{1,0:T(8,128)(2,1)S(1)}, bf16[272,1152]{1,0:T(8,128)(2,1)S(1)}, u32[]{:S(2)}, u32[]{:S(2)}) collective-permute-start(bf16[272,1152]{1,0:T(8,128)(2,1)S(1)} %shard_map.86.refs_1_), channel_id=1, source_target_pairs={{0,1},{1,0},{2,3},{3,2},{4,5},{5,4},{6,7},{7,6},{8,9},{9,8},{10,11... | collective-permute-start | bytes 1880072 | tf_op jit(solution)/shard_map/ppermute | solution.py:23
  42.5 11.2 %collective-permute-start.8 = (bf16[256,1152]{1,0:T(8,128)(2,1)S(1)}, bf16[256,1152]{1,0:T(8,128)(2,1)S(1)}, u32[]{:S(2)}, u32[]{:S(2)}) collective-permute-start(bf16[256,1152]{1,0:T(8,128)(2,1)S(1)} %get-tuple-element.36), channel_id=1, source_target_pairs={{0,1},{1,0},{2,3},{3,2},{4,5},{5,4},{6,7},{7,6},{8,9},{9,8},{10,11... | collective-permute-start | bytes 1769480 | tf_op jit(solution)/shard_map/ppermute | solution.py:23
  45.3 15.6 %collective-permute-start.9 = (bf16[256,1152]{1,0:T(8,128)(2,1)S(1)}, bf16[256,1152]{1,0:T(8,128)(2,1)S(1)}, u32[]{:S(2)}, u32[]{:S(2)}) collective-permute-start(bf16[256,1152]{1,0:T(8,128)(2,1)S(1)} %shard_map.92), channel_id=1, source_target_pairs={{0,4},{4,0},{8,12},{12,8},{16,20},{20,16},{24,28},{28,24},{32,36},... | collective-permute-start | bytes 1769480 | tf_op jit(solution)/shard_map/ppermute | solution.py:21
  48.2 15.2 %collective-permute-start.10 = (bf16[256,1152]{1,0:T(8,128)(2,1)S(1)}, bf16[256,1152]{1,0:T(8,128)(2,1)S(1)}, u32[]{:S(2)}, u32[]{:S(2)}) collective-permute-start(bf16[256,1152]{1,0:T(8,128)(2,1)S(1)} %shard_map.93), channel_id=1, source_target_pairs={{0,128},{4,132},{8,136},{12,140},{16,144},{20,148},{24,152},{28,15... | collective-permute-start | bytes 1769480 | tf_op jit(solution)/shard_map/ppermute | solution.py:21
  56.2 7.5 %collective-permute-start.11 = (bf16[256,1152]{1,0:T(8,128)(2,1)S(1)}, bf16[256,1152]{1,0:T(8,128)(2,1)S(1)}, u32[]{:S(2)}, u32[]{:S(2)}) collective-permute-start(bf16[256,1152]{1,0:T(8,128)(2,1)S(1)} %get-tuple-element.46), channel_id=1, source_target_pairs={{0,1},{1,0},{2,3},{3,2},{4,5},{5,4},{6,7},{7,6},{8,9},{9,8},{10,11... | collective-permute-start | bytes 1769480 | tf_op jit(solution)/shard_map/ppermute | solution.py:23
  59.1 21.2 %collective-permute-start.15 = (bf16[256,1152]{1,0:T(8,128)(2,1)}, bf16[256,1152]{1,0:T(8,128)(2,1)}, u32[]{:S(2)}, u32[]{:S(2)}) collective-permute-start(bf16[256,1152]{1,0:T(8,128)(2,1)} %get-tuple-element.48), channel_id=1, source_target_pairs={{0,4},{4,0},{8,12},{12,8},{16,20},{20,16},{24,28},{28,24},{32,36},... | collective-permute-start | bytes 1769480 | tf_op jit(solution)/shard_map/ppermute | solution.py:21
  59.6 20.7 %collective-permute-start.16 = (bf16[256,1152]{1,0:T(8,128)(2,1)}, bf16[256,1152]{1,0:T(8,128)(2,1)}, u32[]{:S(2)}, u32[]{:S(2)}) collective-permute-start(bf16[256,1152]{1,0:T(8,128)(2,1)} %get-tuple-element.49), channel_id=1, source_target_pairs={{0,128},{4,132},{8,136},{12,140},{16,144},{20,148},{24,152},{28,15... | collective-permute-start | bytes 1769480 | tf_op jit(solution)/shard_map/ppermute | solution.py:21
  64.9 7.7 %collective-permute-start.12 = (f32[8,128]{1,0:T(8,128)S(1)}, f32[8,128]{1,0:T(8,128)S(1)}, u32[]{:S(2)}, u32[]{:S(2)}) collective-permute-start(f32[8,128]{1,0:T(8,128)S(1)} %shard_map.96.refs_0_), channel_id=1, source_target_pairs={{0,2},{1,3},{2,0},{3,1},{4,6},{5,7},{6,4},{7,5},{8,10},{9,11},{10,... | collective-permute-start | bytes 12296 | tf_op jit(solution)/shard_map/ppermute | solution.py:23
  70.5 44.2 %collective-permute-start.22 = (bf16[256,1152]{1,0:T(8,128)(2,1)}, bf16[256,1152]{1,0:T(8,128)(2,1)}, u32[]{:S(2)}, u32[]{:S(2)}) collective-permute-start(bf16[256,1152]{1,0:T(8,128)(2,1)} %shard_map.95.refs_6_), channel_id=1, source_target_pairs={{0,18},{1,19},{2,16},{3,17},{4,22},{5,23},{6,20},{7,21},{8,26},{9,... | collective-permute-start | bytes 1769480 | tf_op jit(solution)/shard_map/ppermute | solution.py:25
  72.6 3.6 %collective-permute-start.13 = (f32[8,128]{1,0:T(8,128)S(1)}, f32[8,128]{1,0:T(8,128)S(1)}, u32[]{:S(2)}, u32[]{:S(2)}) collective-permute-start(f32[8,128]{1,0:T(8,128)S(1)} %shard_map.98.refs_0_), channel_id=1, source_target_pairs={{0,4},{4,0},{8,12},{12,8},{16,20},{20,16},{24,28},{28,24},{32,36},... | collective-permute-start | bytes 12296 | tf_op jit(solution)/shard_map/ppermute | solution.py:21
  76.3 4.0 %collective-permute-start.14 = (f32[8,128]{1,0:T(8,128)S(1)}, f32[8,128]{1,0:T(8,128)S(1)}, u32[]{:S(2)}, u32[]{:S(2)}) collective-permute-start(f32[8,128]{1,0:T(8,128)S(1)} %shard_map.100.refs_0_), channel_id=1, source_target_pairs={{0,16},{4,20},{8,24},{12,28},{16,0},{20,4},{24,8},{28,12},{32,48},... | collective-permute-start | bytes 12296 | tf_op jit(solution)/shard_map/ppermute | solution.py:21
  82.6 2.4 %collective-permute-start.17 = (f32[8,128]{1,0:T(8,128)S(1)}, f32[8,128]{1,0:T(8,128)S(1)}, u32[]{:S(2)}, u32[]{:S(2)}) collective-permute-start(f32[8,128]{1,0:T(8,128)S(1)} %shard_map.104.refs_0_), channel_id=1, source_target_pairs={{0,1},{1,0},{2,3},{3,2},{4,5},{5,4},{6,7},{7,6},{8,9},{9,8},{10,11... | collective-permute-start | bytes 12296 | tf_op jit(solution)/shard_map/ppermute | solution.py:23
  82.6 34.2 %collective-permute-start.23 = (bf16[256,1152]{1,0:T(8,128)(2,1)}, bf16[256,1152]{1,0:T(8,128)(2,1)}, u32[]{:S(2)}, u32[]{:S(2)}) collective-permute-start(bf16[256,1152]{1,0:T(8,128)(2,1)} %shard_map.103.refs_1_), channel_id=1, source_target_pairs={{0,16},{4,20},{8,24},{12,28},{16,0},{20,4},{24,8},{28,12},{32,48},... | collective-permute-start | bytes 1769480 | tf_op jit(solution)/shard_map/ppermute | solution.py:21
  85.0 5.1 %collective-permute-start.18 = (f32[8,128]{1,0:T(8,128)S(1)}, f32[8,128]{1,0:T(8,128)S(1)}, u32[]{:S(2)}, u32[]{:S(2)}) collective-permute-start(f32[8,128]{1,0:T(8,128)S(1)} %shard_map.106.refs_0_), channel_id=1, source_target_pairs={{0,8},{4,12},{8,0},{12,4},{16,24},{20,28},{24,16},{28,20},{32,40},... | collective-permute-start | bytes 12296 | tf_op jit(solution)/shard_map/ppermute | solution.py:21
  90.1 14.8 %collective-permute-start.19 = (f32[8,128]{1,0:T(8,128)S(1)}, f32[8,128]{1,0:T(8,128)S(1)}, u32[]{:S(2)}, u32[]{:S(2)}) collective-permute-start(f32[8,128]{1,0:T(8,128)S(1)} %shard_map.108.refs_0_), channel_id=1, source_target_pairs={{0,32},{4,36},{8,40},{12,44},{16,48},{20,52},{24,56},{28,60},{32,0... | collective-permute-start | bytes 12296 | tf_op jit(solution)/shard_map/ppermute | solution.py:21
  104.9 3.6 %collective-permute-start.20 = (f32[8,128]{1,0:T(8,128)S(1)}, f32[8,128]{1,0:T(8,128)S(1)}, u32[]{:S(2)}, u32[]{:S(2)}) collective-permute-start(f32[8,128]{1,0:T(8,128)S(1)} %shard_map.110.refs_0_), channel_id=1, source_target_pairs={{0,64},{4,68},{8,72},{12,76},{16,80},{20,84},{24,88},{28,92},{32,9... | collective-permute-start | bytes 12296 | tf_op jit(solution)/shard_map/ppermute | solution.py:21
  108.5 5.4 %collective-permute-start.21 = (f32[8,128]{1,0:T(8,128)S(1)}, f32[8,128]{1,0:T(8,128)S(1)}, u32[]{:S(2)}, u32[]{:S(2)}) collective-permute-start(f32[8,128]{1,0:T(8,128)S(1)} %shard_map.112.refs_0_), channel_id=1, source_target_pairs={{0,128},{4,132},{8,136},{12,140},{16,144},{20,148},{24,152},{28,15... | collective-permute-start | bytes 12296 | tf_op jit(solution)/shard_map/ppermute | solution.py:21
  (7 other events, 10.8 us)

commit v2 on v1

v2 whole, which is shorter than its diff:
```python
import functools

import jax
import jax.numpy as jnp
from jax import lax
from jax.experimental import pallas as pl
from jax.experimental.pallas import tpu as pltpu
from jax.sharding import PartitionSpec as P

ROUNDS = 3
LONG = 10_000_000_000
SHORT = 100_000_000
PAD = 16
VMEM = pl.BlockSpec(memory_space=pltpu.VMEM)
SMEM = pl.BlockSpec(memory_space=pltpu.SMEM)
ANY = pl.BlockSpec(memory_space=pl.ANY)
HBM = pl.BlockSpec(memory_space=pltpu.HBM)


def exchange(value, batch_mask, rep_mask=0):
    batch, rep = lax.axis_size("batch"), lax.axis_size("rep")
    if rep_mask == 0:
        return lax.ppermute(value, "batch", [(s, s ^ batch_mask) for s in range(batch)])
    if batch_mask == 0:
        return lax.ppermute(value, "rep", [(s, s ^ rep_mask) for s in range(rep)])
    mask = batch_mask * rep + rep_mask
    return lax.ppermute(value, ("batch", "rep"), [(s, s ^ mask) for s in range(batch * rep)])


def pack_kernel(starts, image_ref, weight_ref, *refs):
    out_refs, held, copied = refs[:-2], refs[-2], refs[-1]
    counts = [out_ref.shape[0] - PAD for out_ref in out_refs]
    copies = [pltpu.make_async_copy(weight_ref, held, copied.at[0])]
    for index, (start, count, out_ref) in enumerate(zip(starts, counts, out_refs)):
        source = image_ref.at[pl.ds(start, count)]
        target = out_ref.at[pl.ds(0, count)]
        copies.append(pltpu.make_async_copy(source, target, copied.at[index + 1]))
    for copy in copies:
        copy.start()
    copies[0].wait()
    for start, count, out_ref in zip(starts, counts, out_refs):
        place = lax.broadcasted_iota(jnp.int32, (PAD, count), 0)
        rest = held[:, start : start + count]
        tail = jnp.zeros((PAD, count), jnp.float32)
        for part_index in range(3):
            part = rest.astype(jnp.bfloat16).astype(jnp.float32)
            rest = rest - part
            tail = jnp.where(place == part_index, part, tail)
        out_ref[count:, :count] = tail.astype(jnp.bfloat16)
        out_ref[count:, count:] = jnp.zeros((PAD, out_ref.shape[1] - count), jnp.bfloat16)
    for copy in copies[1:]:
        copy.wait()


def pack_weights(images, weight, ranges):
    rows, width = images.shape
    return pl.pallas_call(
        functools.partial(pack_kernel, [start for start, _ in ranges]),
        out_shape=[jax.ShapeDtypeStruct((count + PAD, width), images.dtype) for _, count in ranges],
        in_specs=[HBM, HBM],
        out_specs=[VMEM] * len(ranges),
        scratch_shapes=[
            pltpu.VMEM((1, rows), jnp.float32),
            pltpu.SemaphoreType.DMA((len(ranges) + 1,)),
        ],
        cost_estimate=pl.CostEstimate(flops=1, bytes_accessed=1, transcendentals=0),
        compiler_params=pltpu.CompilerParams(vmem_limit_bytes=4 * 2**20),
    )(images, weight[None])


def held_back(value, *after):
    return lax.optimization_barrier((value, *after))[0]


def mark_kernel(*refs):
    refs[-1][...] = jnp.zeros_like(refs[-1])


def beside(*values, flops=LONG):
    return pl.pallas_call(
        mark_kernel,
        out_shape=jax.ShapeDtypeStruct((8, 128), jnp.float32),
        in_specs=[ANY] * len(values),
        out_specs=VMEM,
        compiler_params=pltpu.CompilerParams(vmem_limit_bytes=2**20),
        cost_estimate=pl.CostEstimate(flops=flops, bytes_accessed=1, transcendentals=0),
    )(*values)


def add_kernel(count, pairs, *refs):
    values = [ref[...].astype(jnp.float32) for ref in refs[:count]]
    if pairs:
        values = [values[0] + values[1], values[2] + values[3]]
    total = values[0]
    for value in values[1:]:
        total = total + value
    refs[-1][...] = total.astype(refs[-1].dtype)


def add_up(kind, values, after=(), pairs=False):
    return pl.pallas_call(
        functools.partial(add_kernel, len(values), pairs),
        out_shape=jax.ShapeDtypeStruct(values[0].shape, kind),
        in_specs=[VMEM] * len(values) + [ANY] * len(after),
        out_specs=VMEM,
        compiler_params=pltpu.CompilerParams(vmem_limit_bytes=8 * 2**20),
        cost_estimate=pl.CostEstimate(flops=1, bytes_accessed=1, transcendentals=0),
    )(*values, *after)


def all_sum_step(value, batch_mask, rep_mask, after=()):
    received = exchange(value, batch_mask, rep_mask)
    return add_up(value.dtype, [value, received], (beside(value, *after, flops=SHORT),))


def score_block(scores, weight, scale, bias, positive):
    logits = scale * scores + bias
    small = jnp.exp(-jnp.abs(logits))
    total = 1.0 + small
    inverse = 1.0 / total
    chance = jnp.where(logits >= 0, inverse, small * inverse)
    lost = (small - (total - 1.0)) * inverse
    penalty = jnp.maximum(logits, 0.0) + (jnp.log(total) + lost)
    if positive:
        rows = lax.broadcasted_iota(jnp.int32, scores.shape, 0)
        same = rows == lax.broadcasted_iota(jnp.int32, scores.shape, 1)
        chance = chance - jnp.where(same, 1.0, 0.0)
        penalty = penalty - jnp.where(same, logits, 0.0)
    terms = (penalty, chance * scores, chance)
    sums = [jnp.sum(term, axis=0, keepdims=True) for term in terms]
    return (weight * chance).astype(jnp.bfloat16), [weight * value for value in sums]


def store_sums(sums_out, totals, scale):
    half = totals[0].shape[1] // 2
    totals = [totals[0], totals[1] * scale, totals[2]]
    folded = [total[:, :half] + total[:, half:] for total in totals]
    sums_out[...] = jnp.concatenate(folded + [jnp.zeros((8 - len(folded), half), jnp.float32)])


def pair_kernel(
    image_pieces, text_pieces, after, positive, add_text, add_image, text_types, image_types, *refs
):
    refs = list(refs)
    take = lambda counts: [[refs.pop(0) for _ in range(count)] for count in counts]
    images, texts = len(image_pieces), len(text_pieces)
    scalars = refs.pop(0)
    image_refs, text_refs = take(image_pieces), take(text_pieces)
    add_text_refs = take(add_text)
    add_image_refs = take(add_image)
    del refs[:after]
    text_outs = [refs.pop(0) for _ in range(texts)]
    image_outs = take([len(kinds) for kinds in image_types])
    sums_out, coupling, held = refs
    rows = coupling.shape[-1]
    scale, bias = scalars[0], scalars[1]
    totals = [jnp.zeros((1, rows), jnp.float32) for _ in range(3)]

    slot, image_blocks, text_blocks, weights = 0, [], [], []
    for pieces in text_refs:
        if len(pieces) == 1:
            text_blocks.append(pieces[0])
            continue
        start = 0
        for piece in pieces:
            held[slot, start : start + piece.shape[0]] = piece[...]
            start += piece.shape[0]
        text_blocks.append(held.at[slot])
        slot += 1
    for pieces in image_refs:
        start, parts = 0, []
        for piece in pieces:
            count = piece.shape[0] - PAD
            held[slot, start : start + count] = piece[:count]
            tail = piece[count:, :count].astype(jnp.float32)
            parts.append(tail[0:1] + tail[1:2] + tail[2:3])
            start += count
        image_blocks.append(held.at[slot])
        weights.append(parts[0] if len(parts) == 1 else jnp.concatenate(parts, axis=1))
        slot += 1

    for i, image_ref in enumerate(image_blocks):
        weight = weights[i]
        for j, text_ref in enumerate(text_blocks):
            scores = lax.dot_general(
                text_ref[...],
                image_ref[...],
                (((1,), (1,)), ((), ())),
                preferred_element_type=jnp.float32,
            )
            coupling[i, j], sums = score_block(
                scores, weight, scale, bias, positive and i == 0 and j == 0
            )
            totals = [total + value for total, value in zip(totals, sums)]
    store_sums(sums_out, totals, scale)
    for i in range(images):
        value = None
        for j in range(texts):
            term = lax.dot_general(
                coupling[i, j],
                text_blocks[j][...],
                (((0,), (0,)), ((), ())),
                preferred_element_type=jnp.float32,
            )
            value = term if value is None else value + term
        value = value * scale
        for ref in add_image_refs[i]:
            value = value + ref[...].astype(jnp.float32)
        image_outs[i][0][...] = value.astype(image_types[i][0])
    for j in range(texts):
        value = None
        for i in range(images):
            term = jnp.dot(
                coupling[i, j], image_blocks[i][...], preferred_element_type=jnp.float32
            )
            value = term if value is None else value + term
        value = value * scale
        for ref in add_text_refs[j]:
            value = value + ref[...].astype(jnp.float32)
        text_outs[j][...] = value.astype(text_types[j])


def pair_terms(
    scalars,
    images,
    texts,
    text_types,
    image_types,
    add_text=None,
    add_image=None,
    positive=False,
    after=(),
    flops=1,
):
    add_text = add_text or [[]] * len(texts)
    add_image = add_image or [[]] * len(images)
    rows, width = sum(piece.shape[0] for piece in texts[0]), texts[0][0].shape[1]
    blocks = len(images) * len(texts)
    operands = [piece for pieces in list(images) + list(texts) for piece in pieces]
    operands += [value for values in add_text for value in values]
    operands += [value for values in add_image for value in values]
    image_shapes = [
        jax.ShapeDtypeStruct((rows // len(kinds), width), kind) for kinds in image_types for kind in kinds
    ]
    held = len(images) + sum(len(pieces) > 1 for pieces in texts)
    outs = pl.pallas_call(
        functools.partial(
            pair_kernel,
            [len(pieces) for pieces in images],
            [len(pieces) for pieces in texts],
            len(after),
            positive,
            [len(values) for values in add_text],
            [len(values) for values in add_image],
            text_types,
            image_types,
        ),
        out_shape=[jax.ShapeDtypeStruct((rows, width), kind) for kind in text_types]
        + image_shapes
        + [jax.ShapeDtypeStruct((8, rows // 2), jnp.float32)],
        in_specs=[SMEM] + [VMEM] * len(operands) + [ANY] * len(after),
        out_specs=[VMEM] * (len(texts) + len(image_shapes) + 1),
        scratch_shapes=[
            pltpu.VMEM((len(images), len(texts), rows, rows), jnp.bfloat16),
            pltpu.VMEM((held, rows, width), jnp.bfloat16),
        ],
        compiler_params=pltpu.CompilerParams(vmem_limit_bytes=16 * 2**20),
        cost_estimate=pl.CostEstimate(
            flops=flops, bytes_accessed=1, transcendentals=0
        ),
    )(scalars, *operands, *after)
    image_outs, place = [], len(texts)
    for kinds in image_types:
        image_outs.append(outs[place : place + len(kinds)])
        place += len(kinds)
    return outs[: len(texts)], image_outs, outs[-1]


def on_device(images, caption_vectors, sample_weight, natural_odds_factor, bias):
    f32, bf16 = jnp.float32, jnp.bfloat16
    groups, rep_count = lax.axis_size("batch"), lax.axis_size("rep")
    rows = images.shape[0]
    bits = groups.bit_length() - 1
    x_bit, z_bit, y_bit = [1 << (step * (bits - 1) // (ROUNDS - 1)) for step in range(ROUNDS)]
    core, far = 1, rep_count // 2
    barrier = lax.optimization_barrier

    scalars = jnp.concatenate([jnp.exp(natural_odds_factor), bias])
    texts = caption_vectors
    texts_z = exchange(texts, z_bit)
    texts_x = exchange(texts, x_bit)
    texts_y = exchange(texts, y_bit)
    (own,) = pack_weights(images, sample_weight, [(0, rows)])
    other = exchange(own, 0, core)

    away = exchange(held_back(own, texts_z), z_bit, far)
    texts_zx = exchange(texts_z, x_bit)
    texts_zy = exchange(texts_z, y_bit)
    (d0, dz, dx, dy), ((image_own,), (image_other,)), sums_a = pair_terms(
        scalars,
        [[own], [other]],
        [[texts], [texts_z], [texts_x], [texts_y]],
        [f32, f32, bf16, bf16],
        [[bf16], [bf16]],
        positive=True,
    )
    image_back = exchange(image_other, 0, core)
    image_near = add_up(bf16, [image_own, image_back])

    away = held_back(away, image_near, texts_zx, texts_zy)
    away_other = exchange(away, 0, core)
    dx_back = exchange(held_back(dx, texts_zx), x_bit)
    dy_back = exchange(held_back(dy, texts_zy), y_bit)
    (dzx, dzy), (far_own,), sums_b = pair_terms(
        scalars,
        [[away]],
        [[texts_zx], [texts_zy]],
        [f32, f32],
        [[f32]],
        flops=LONG,
    )
    (d0, dz, dzx, dzy), ((far_other,),), sums_c = pair_terms(
        scalars,
        [[away_other]],
        [[texts], [texts_z], [texts_zx], [texts_zy]],
        [f32, f32, bf16, bf16],
        [[bf16]],
        add_text=[[d0], [dz], [dzx], [dzy]],
        after=(sums_b,),
    )
    near_back = exchange(far_other, 0, core)
    dzx_back = exchange(dzx, x_bit)
    dzy_back = exchange(dzy, y_bit)
    (d0, dz), ((far_total,),), sums_d = pair_terms(
        scalars,
        [[away]],
        [[texts], [texts_z]],
        [bf16, f32],
        [[bf16]],
        add_text=[[d0, dx_back, dy_back], [dz]],
        add_image=[[*far_own, near_back]],
        after=(sums_c,),
    )
    image_away = exchange(far_total, z_bit, far)

    sums = add_up(f32, [sums_a, sums_b, sums_c, sums_d])
    sums = all_sum_step(sums, z_bit, 0)
    sums = all_sum_step(sums, 0, far)
    dz_total = add_up(bf16, [dz, dzx_back, dzy_back], (sums,))
    dz_back = exchange(dz_total, z_bit)
    sums = all_sum_step(held_back(sums, dz_total), 0, core)
    sums = all_sum_step(sums, 3 * x_bit, 0)
    sums = all_sum_step(sums, 2 * x_bit, 0)
    sums = all_sum_step(sums, y_bit // 2, 0)
    sums = all_sum_step(sums, y_bit // 2 * 3, 0)
    received = exchange(sums, 2 * z_bit)
    grad_images = (image_near.astype(f32) + image_away).astype(bf16)
    sums = add_up(f32, [sums, received], (grad_images,))
    totals = jnp.sum(sums, axis=1)

    pair_count = float(rows * rep_count * groups * rows * rep_count * (ROUNDS + 1))
    loss = totals[0:1] / pair_count
    grad_scalars = totals[1:3] / pair_count
    grad_texts = (d0.astype(f32) + dz_back).astype(bf16)
    return loss, grad_scalars, grad_images, grad_texts


def solution(mesh):
    in_specs = (P(("batch", "rep"), None), P(("batch", "rep"), None), P(("batch", "rep")), P(), P())
    out_specs = (P(), P(), P(("batch", "rep"), None), P(("batch", "rep"), None))
    return jax.shard_map(
        on_device, mesh=mesh, in_specs=in_specs, out_specs=out_specs, check_vma=False
    )
```

time: 121 us -> 108 us (0.89)
  Pallas kernels: 23.8 us -> 15.1 us
  waiting for transfers between devices: 48.4 us -> 43.2 us
    ppermute x16, waiting for transfers between devices: 47.7 us -> 30.3 us  [exchange(): lax.ppermute(value, 'batch', [(s, s ^ batch_mask) for s in range(batch)])]
    pallas_call x33 -> x23, Pallas kernels: 23.8 us -> 15.1 us  [the longest x4 14.5 us: pair_terms(): pl.pallas_call(functools.partial(pair_kernel, [len(pieces) for pieces in...]
    ppermute x2, waiting for transfers between devices: 0.01 us -> 6.59 us  [exchange(): lax.ppermute(value, ('batch', 'rep'), [(s, s ^ mask) for s in range(batch...]
    ppermute x6, waiting for transfers between devices: 0.78 us -> 6.3 us  [exchange(): return lax.ppermute(value, 'rep', [(s, s ^ rep_mask) for s in range(rep)])]
    ppermute x16, starting transfers between devices: 29 us -> 34.1 us  [exchange(): lax.ppermute(value, 'batch', [(s, s ^ batch_mask) for s in range(batch)])]
    ppermute x6, starting transfers between devices: 6.36 us -> 2.45 us  [exchange(): return lax.ppermute(value, 'rep', [(s, s ^ rep_mask) for s in range(rep)])]
    unnamed x14 -> x8, local copies, waits for them, and re-layouts: 2.77 us -> 1.75 us
  transfers between devices with their start and end apart: 24 -> 24, of which waited for: 11 -> 10; matrix products, arithmetic and copies ran while one was open for 1% -> 1% of each run, Pallas kernels for 18% -> 14%
where the time goes in v2:
time: 108 us; the launch traced here: 107 us
  waiting for transfers between devices  43.2 us (40%)
  starting transfers between devices  41.4 us (38%)
  Pallas kernels  15.1 us (14%)
  between operations  3.31 us (3%)
  other arithmetic  1.9 us (2%)
  local copies, waits for them, and re-layouts  1.75 us (2%)
    ppermute x16, starting transfers between devices, exchange(): lax.ppermute(value, 'batch', [(s, s ^ batch_mask) for s in range(batch)])  34.1 us
    ppermute x16, waiting for transfers between devices, exchange(): lax.ppermute(value, 'batch', [(s, s ^ batch_mask) for s in range(batch)])  30.3 us
    pallas_call x4, Pallas kernels, pair_terms(): pl.pallas_call(functools.partial(pair_kernel, [len(pieces) for pieces in...  14.5 us
    ppermute x2, waiting for transfers between devices, exchange(): lax.ppermute(value, ('batch', 'rep'), [(s, s ^ mask) for s in range(batch...  6.59 us
    ppermute x6, waiting for transfers between devices, exchange(): return lax.ppermute(value, 'rep', [(s, s ^ rep_mask) for s in range(rep)])  6.3 us
    ppermute x2, starting transfers between devices, exchange(): lax.ppermute(value, ('batch', 'rep'), [(s, s ^ mask) for s in range(batch...  4.86 us
    ppermute x6, starting transfers between devices, exchange(): return lax.ppermute(value, 'rep', [(s, s ^ rep_mask) for s in range(rep)])  2.45 us
  transfers between devices with their start and end apart: 24, of which 10 were waited for; matrix products, arithmetic and copies ran while one was open for 1% of the time, Pallas kernels for 14%

profile of v2, /device:TPU:64, one launch (start us, length us, event | category | flops | bytes accessed | tf_op | source)
XLA Modules:
  0.0 106.6 jit_solution(12889398711448667667)
XLA Ops:
  0.6 2.0 %collective-permute-start.1 = (bf16[256,1152]{1,0:T(8,128)(2,1)}, bf16[256,1152]{1,0:T(8,128)(2,1)S(1)}, u32[]{:S(2)}, u32[]{:S(2)}) collective-permute-start(bf16[256,1152]{1,0:T(8,128)(2,1)} %refs_2_.3), channel_id=1, source_target_pairs={{0,16},{4,20},{8,24},{12,28},{16,0},{20,4},{24,8},{28,12},{32,48},... | collective-permute-start | bytes 1769480 | tf_op jit(solution)/shard_map/ppermute | solution.py:23
  2.6 3.2 %collective-permute-start.3 = (bf16[256,1152]{1,0:T(8,128)(2,1)}, bf16[256,1152]{1,0:T(8,128)(2,1)S(1)}, u32[]{:S(2)}, u32[]{:S(2)}) collective-permute-start(bf16[256,1152]{1,0:T(8,128)(2,1)} %refs_2_.3), channel_id=1, source_target_pairs={{0,128},{4,132},{8,136},{12,140},{16,144},{20,148},{24,152},{28,15... | collective-permute-start | bytes 1769480 | tf_op jit(solution)/shard_map/ppermute | solution.py:23
  7.9 1.6 %collective-permute-start.2 = (bf16[256,1152]{1,0:T(8,128)(2,1)S(1)}, bf16[256,1152]{1,0:T(8,128)(2,1)S(1)}, u32[]{:S(2)}, u32[]{:S(2)}) collective-permute-start(bf16[256,1152]{1,0:T(8,128)(2,1)S(1)} %copy-done), channel_id=1, source_target_pairs={{0,4},{4,0},{8,12},{12,8},{16,20},{20,16},{24,28},{28,24},{32,36},... | collective-permute-start | bytes 1769480 | tf_op jit(solution)/shard_map/ppermute | solution.py:23
  10.8 5.4 %collective-permute-done.1.refs_4_.refs_3_ = bf16[256,1152]{1,0:T(8,128)(2,1)S(1)} collective-permute-done((bf16[256,1152]{1,0:T(8,128)(2,1)}, bf16[256,1152]{1,0:T(8,128)(2,1)S(1)}, u32[]{:S(2)}, u32[]{:S(2)}) %collective-permute-start.1) | collective-permute-done | bytes 589856 | tf_op jit(solution)/shard_map/ppermute | solution.py:23
  16.2 4.8 %collective-permute-start.4 = (bf16[272,1152]{1,0:T(8,128)(2,1)S(1)}, bf16[272,1152]{1,0:T(8,128)(2,1)S(1)}, u32[]{:S(2)}, u32[]{:S(2)}) collective-permute-start(bf16[272,1152]{1,0:T(8,128)(2,1)S(1)} %shard_map.84.refs_1_), channel_id=1, source_target_pairs={{0,18},{1,19},{2,16},{3,17},{4,22},{5,23},{6,20},{7,21},{8,26},{9,... | collective-permute-start | bytes 1880072 | tf_op jit(solution)/shard_map/ppermute | solution.py:27
  21.0 3.2 %collective-permute-start.7 = (bf16[256,1152]{1,0:T(8,128)(2,1)S(1)}, bf16[256,1152]{1,0:T(8,128)(2,1)S(1)}, u32[]{:S(2)}, u32[]{:S(2)}) collective-permute-start(bf16[256,1152]{1,0:T(8,128)(2,1)S(1)} %collective-permute-done.1.refs_4_.refs_3_), channel_id=1, source_target_pairs={{0,128},{4,132},{8,136},{12,140},{16,144},{20,148},{24,152},{28,15... | collective-permute-start | bytes 1769480 | tf_op jit(solution)/shard_map/ppermute | solution.py:23
  25.7 6.3 %shard_map.85 = (f32[256,1152]{1,0:T(8,128)S(1)}, f32[256,1152]{1,0:T(8,128)S(1)}, bf16[256,1152]{1,0:T(8,128)(2,1)S(1)}, bf16[256,1152]{1,0:T(8,128)(2,1)S(1)},...) custom-call(f32[2]{0:T(128)S(1)} %pad_maximum_fusion.refs_0_, ...), custom_call_target="tpu_custom_call" | custom-call | flops 1 | bytes 1 | tf_op jit(solution)/shard_map/pallas_call | solution.py:246
  32.1 5.7 %collective-permute-done.6.refs_2_.refs_4_ = bf16[256,1152]{1,0:T(8,128)(2,1)S(1)} collective-permute-done((bf16[256,1152]{1,0:T(8,128)(2,1)S(1)}, bf16[256,1152]{1,0:T(8,128)(2,1)S(1)}, u32[]{:S(2)}, u32[]{:S(2)}) %collective-permute-start.6) | collective-permute-done | bytes 589856 | tf_op jit(solution)/shard_map/ppermute | solution.py:23
  37.8 1.8 %collective-permute-start.10 = (bf16[256,1152]{1,0:T(8,128)(2,1)S(1)}, bf16[256,1152]{1,0:T(8,128)(2,1)S(1)}, u32[]{:S(2)}, u32[]{:S(2)}) collective-permute-start(bf16[256,1152]{1,0:T(8,128)(2,1)S(1)} %get-tuple-element.45), channel_id=1, source_target_pairs={{0,128},{4,132},{8,136},{12,140},{16,144},{20,148},{24,152},{28,15... | collective-permute-start | bytes 1769480 | tf_op jit(solution)/shard_map/ppermute | solution.py:23
  41.2 6.6 %collective-permute-done.4.refs_1_ = bf16[272,1152]{1,0:T(8,128)(2,1)S(1)} collective-permute-done((bf16[272,1152]{1,0:T(8,128)(2,1)S(1)}, bf16[272,1152]{1,0:T(8,128)(2,1)S(1)}, u32[]{:S(2)}, u32[]{:S(2)}) %collective-permute-start.4) | collective-permute-done | bytes 626720 | tf_op jit(solution)/shard_map/ppermute | solution.py:27
  47.8 2.3 %shard_map.87 = (f32[256,1152]{1,0:T(8,128)S(1)}, f32[256,1152]{1,0:T(8,128)S(1)}, f32[256,1152]{1,0:T(8,128)S(1)}, f32[8,128]{1,0:T(8,128)S(1)}) custom-call(f32[2]{0:T(128)S(1)} %pad_maximum_fusion.refs_0_, bf16[272,1152]{1,0:T(8,128)(2,1)S(1)} %collective-permute-done.4.refs_1_, bf16[256,1152]{1,0:T(8,128)(2,1)S(1)} %collective-permute-done.6.refs_2_.refs_4_, ...), custom_call_target="tpu_custom_call" | custom-call | flops 10000000000 | bytes 1 | tf_op jit(solution)/shard_map/pallas_call | solution.py:246
  50.1 3.5 %shard_map.88 = (f32[256,1152]{1,0:T(8,128)S(1)}, f32[256,1152]{1,0:T(8,128)S(1)}, bf16[256,1152]{1,0:T(8,128)(2,1)S(1)}, bf16[256,1152]{1,0:T(8,128)(2,1)S(1)},...) custom-call(f32[2]{0:T(128)S(1)} %pad_maximum_fusion.refs_0_, bf16[272,1152]{1,0:T(8,128)(2,1)S(1)} %collective-permute-done.8.refs_1_, ...), custom_call_target="tpu_custom_call" | custom-call | flops 1 | bytes 1 | tf_op jit(solution)/shard_map/pallas_call | solution.py:246
  55.7 3.2 %collective-permute-start.15 = (bf16[256,1152]{1,0:T(8,128)(2,1)S(1)}, bf16[256,1152]{1,0:T(8,128)(2,1)S(1)}, u32[]{:S(2)}, u32[]{:S(2)}) collective-permute-start(bf16[256,1152]{1,0:T(8,128)(2,1)S(1)} %get-tuple-element.52), channel_id=1, source_target_pairs={{0,128},{4,132},{8,136},{12,140},{16,144},{20,148},{24,152},{28,15... | collective-permute-start | bytes 1769480 | tf_op jit(solution)/shard_map/ppermute | solution.py:23
  58.9 2.4 %shard_map.89 = (bf16[256,1152]{1,0:T(8,128)(2,1)S(1)}, f32[256,1152]{1,0:T(8,128)S(1)}, bf16[256,1152]{1,0:T(8,128)(2,1)S(1)}, f32[8,128]{1,0:T(8,128)S(1)}) custom-call(f32[2]{0:T(128)S(1)} %pad_maximum_fusion.refs_0_, bf16[272,1152]{1,0:T(8,128)(2,1)S(1)} %collective-permute-done.4.refs_1_, bf16[256,1152]{1,0:T(8,128)(2,1)S(1)} %copy-done, ...), custom_call_target="tpu_custom_call" | custom-call | flops 1 | bytes 1 | tf_op jit(solution)/shard_map/pallas_call | solution.py:246
  61.5 5.6 %collective-permute-start.12 = (f32[8,128]{1,0:T(8,128)S(1)}, f32[8,128]{1,0:T(8,128)S(1)}, u32[]{:S(2)}, u32[]{:S(2)}) collective-permute-start(f32[8,128]{1,0:T(8,128)S(1)} %shard_map.90.refs_0_), channel_id=1, source_target_pairs={{0,16},{4,20},{8,24},{12,28},{16,0},{20,4},{24,8},{28,12},{32,48},... | collective-permute-start | bytes 12296 | tf_op jit(solution)/shard_map/ppermute | solution.py:23
  67.0 1.6 %collective-permute-done.12.refs_1_ = f32[8,128]{1,0:T(8,128)S(1)} collective-permute-done((f32[8,128]{1,0:T(8,128)S(1)}, f32[8,128]{1,0:T(8,128)S(1)}, u32[]{:S(2)}, u32[]{:S(2)}) %collective-permute-start.12) | collective-permute-done | bytes 4128 | tf_op jit(solution)/shard_map/ppermute | solution.py:23
  70.2 6.3 %collective-permute-done.13.refs_1_ = f32[8,128]{1,0:T(8,128)S(1)} collective-permute-done((f32[8,128]{1,0:T(8,128)S(1)}, f32[8,128]{1,0:T(8,128)S(1)}, u32[]{:S(2)}, u32[]{:S(2)}) %collective-permute-start.13) | collective-permute-done | bytes 4128 | tf_op jit(solution)/shard_map/ppermute | solution.py:25
  76.8 2.3 %collective-permute-start.23 = (bf16[256,1152]{1,0:T(8,128)(2,1)S(1)}, bf16[256,1152]{1,0:T(8,128)(2,1)S(1)}, u32[]{:S(2)}, u32[]{:S(2)}) collective-permute-start(bf16[256,1152]{1,0:T(8,128)(2,1)S(1)} %shard_map.95), channel_id=1, source_target_pairs={{0,16},{4,20},{8,24},{12,28},{16,0},{20,4},{24,8},{28,12},{32,48},... | collective-permute-start | bytes 1769480 | tf_op jit(solution)/shard_map/ppermute | solution.py:23
  79.1 2.1 %collective-permute-start.17 = (f32[8,128]{1,0:T(8,128)S(1)}, f32[8,128]{1,0:T(8,128)S(1)}, u32[]{:S(2)}, u32[]{:S(2)}) collective-permute-start(f32[8,128]{1,0:T(8,128)S(1)} %shard_map.97.refs_0_), channel_id=1, source_target_pairs={{0,12},{4,8},{8,4},{12,0},{16,28},{20,24},{24,20},{28,16},{32,44},... | collective-permute-start | bytes 12296 | tf_op jit(solution)/shard_map/ppermute | solution.py:23
  81.2 2.7 %collective-permute-done.17.refs_1_ = f32[8,128]{1,0:T(8,128)S(1)} collective-permute-done((f32[8,128]{1,0:T(8,128)S(1)}, f32[8,128]{1,0:T(8,128)S(1)}, u32[]{:S(2)}, u32[]{:S(2)}) %collective-permute-start.17) | collective-permute-done | bytes 4128 | tf_op jit(solution)/shard_map/ppermute | solution.py:23
  85.4 3.6 %collective-permute-done.18.refs_1_ = f32[8,128]{1,0:T(8,128)S(1)} collective-permute-done((f32[8,128]{1,0:T(8,128)S(1)}, f32[8,128]{1,0:T(8,128)S(1)}, u32[]{:S(2)}, u32[]{:S(2)}) %collective-permute-start.18) | collective-permute-done | bytes 4128 | tf_op jit(solution)/shard_map/ppermute | solution.py:23
  89.7 2.9 %collective-permute-done.19.refs_1_ = f32[8,128]{1,0:T(8,128)S(1)} collective-permute-done((f32[8,128]{1,0:T(8,128)S(1)}, f32[8,128]{1,0:T(8,128)S(1)}, u32[]{:S(2)}, u32[]{:S(2)}) %collective-permute-start.19) | collective-permute-done | bytes 4128 | tf_op jit(solution)/shard_map/ppermute | solution.py:23
  93.7 3.8 %collective-permute-done.20.refs_1_ = f32[8,128]{1,0:T(8,128)S(1)} collective-permute-done((f32[8,128]{1,0:T(8,128)S(1)}, f32[8,128]{1,0:T(8,128)S(1)}, u32[]{:S(2)}, u32[]{:S(2)}) %collective-permute-start.20) | collective-permute-done | bytes 4128 | tf_op jit(solution)/shard_map/ppermute | solution.py:23
  99.2 4.6 %collective-permute-done.21.refs_1_ = f32[8,128]{1,0:T(8,128)S(1)} collective-permute-done((f32[8,128]{1,0:T(8,128)S(1)}, f32[8,128]{1,0:T(8,128)S(1)}, u32[]{:S(2)}, u32[]{:S(2)}) %collective-permute-start.21) | collective-permute-done | bytes 4128 | tf_op jit(solution)/shard_map/ppermute | solution.py:23
  (60 shorter events, 16.0 us)
Async XLA Ops:
  0.6 15.5 %collective-permute-start.1 = (bf16[256,1152]{1,0:T(8,128)(2,1)}, bf16[256,1152]{1,0:T(8,128)(2,1)S(1)}, u32[]{:S(2)}, u32[]{:S(2)}) collective-permute-start(bf16[256,1152]{1,0:T(8,128)(2,1)} %refs_2_.3), channel_id=1, source_target_pairs={{0,16},{4,20},{8,24},{12,28},{16,0},{20,4},{24,8},{28,12},{32,48},... | collective-permute-start | bytes 1769480 | tf_op jit(solution)/shard_map/ppermute | solution.py:23
  2.6 21.5 %collective-permute-start.3 = (bf16[256,1152]{1,0:T(8,128)(2,1)}, bf16[256,1152]{1,0:T(8,128)(2,1)S(1)}, u32[]{:S(2)}, u32[]{:S(2)}) collective-permute-start(bf16[256,1152]{1,0:T(8,128)(2,1)} %refs_2_.3), channel_id=1, source_target_pairs={{0,128},{4,132},{8,136},{12,140},{16,144},{20,148},{24,152},{28,15... | collective-permute-start | bytes 1769480 | tf_op jit(solution)/shard_map/ppermute | solution.py:23
  7.7 18.0 %collective-permute-start = (bf16[272,1152]{1,0:T(8,128)(2,1)S(1)}, bf16[272,1152]{1,0:T(8,128)(2,1)S(1)}, u32[]{:S(2)}, u32[]{:S(2)}) collective-permute-start(bf16[272,1152]{1,0:T(8,128)(2,1)S(1)} %shard_map.84.refs_1_), channel_id=1, source_target_pairs={{0,1},{1,0},{2,3},{3,2},{4,5},{5,4},{6,7},{7,6},{8,9},{9,8},{10,11... | collective-permute-start | bytes 1880072 | tf_op jit(solution)/shard_map/ppermute | solution.py:25
  7.9 17.9 %collective-permute-start.2 = (bf16[256,1152]{1,0:T(8,128)(2,1)S(1)}, bf16[256,1152]{1,0:T(8,128)(2,1)S(1)}, u32[]{:S(2)}, u32[]{:S(2)}) collective-permute-start(bf16[256,1152]{1,0:T(8,128)(2,1)S(1)} %copy-done), channel_id=1, source_target_pairs={{0,4},{4,0},{8,12},{12,8},{16,20},{20,16},{24,28},{28,24},{32,36},... | collective-permute-start | bytes 1769480 | tf_op jit(solution)/shard_map/ppermute | solution.py:23
  16.2 31.6 %collective-permute-start.4 = (bf16[272,1152]{1,0:T(8,128)(2,1)S(1)}, bf16[272,1152]{1,0:T(8,128)(2,1)S(1)}, u32[]{:S(2)}, u32[]{:S(2)}) collective-permute-start(bf16[272,1152]{1,0:T(8,128)(2,1)S(1)} %shard_map.84.refs_1_), channel_id=1, source_target_pairs={{0,18},{1,19},{2,16},{3,17},{4,22},{5,23},{6,20},{7,21},{8,26},{9,... | collective-permute-start | bytes 1880072 | tf_op jit(solution)/shard_map/ppermute | solution.py:27
  21.0 16.8 %collective-permute-start.7 = (bf16[256,1152]{1,0:T(8,128)(2,1)S(1)}, bf16[256,1152]{1,0:T(8,128)(2,1)S(1)}, u32[]{:S(2)}, u32[]{:S(2)}) collective-permute-start(bf16[256,1152]{1,0:T(8,128)(2,1)S(1)} %collective-permute-done.1.refs_4_.refs_3_), channel_id=1, source_target_pairs={{0,128},{4,132},{8,136},{12,140},{16,144},{20,148},{24,152},{28,15... | collective-permute-start | bytes 1769480 | tf_op jit(solution)/shard_map/ppermute | solution.py:23
  24.2 13.6 %collective-permute-start.6 = (bf16[256,1152]{1,0:T(8,128)(2,1)S(1)}, bf16[256,1152]{1,0:T(8,128)(2,1)S(1)}, u32[]{:S(2)}, u32[]{:S(2)}) collective-permute-start(bf16[256,1152]{1,0:T(8,128)(2,1)S(1)} %collective-permute-done.1.refs_4_.refs_3_), channel_id=1, source_target_pairs={{0,4},{4,0},{8,12},{12,8},{16,20},{20,16},{24,28},{28,24},{32,36},... | collective-permute-start | bytes 1769480 | tf_op jit(solution)/shard_map/ppermute | solution.py:23
  32.0 9.1 %collective-permute-start.5 = (bf16[256,1152]{1,0:T(8,128)(2,1)S(1)}, bf16[256,1152]{1,0:T(8,128)(2,1)S(1)}, u32[]{:S(2)}, u32[]{:S(2)}) collective-permute-start(bf16[256,1152]{1,0:T(8,128)(2,1)S(1)} %get-tuple-element.33), channel_id=1, source_target_pairs={{0,1},{1,0},{2,3},{3,2},{4,5},{5,4},{6,7},{7,6},{8,9},{9,8},{10,11... | collective-permute-start | bytes 1769480 | tf_op jit(solution)/shard_map/ppermute | solution.py:25
  37.8 21.1 %collective-permute-start.10 = (bf16[256,1152]{1,0:T(8,128)(2,1)S(1)}, bf16[256,1152]{1,0:T(8,128)(2,1)S(1)}, u32[]{:S(2)}, u32[]{:S(2)}) collective-permute-start(bf16[256,1152]{1,0:T(8,128)(2,1)S(1)} %get-tuple-element.45), channel_id=1, source_target_pairs={{0,128},{4,132},{8,136},{12,140},{16,144},{20,148},{24,152},{28,15... | collective-permute-start | bytes 1769480 | tf_op jit(solution)/shard_map/ppermute | solution.py:23
  39.6 19.3 %collective-permute-start.9 = (bf16[256,1152]{1,0:T(8,128)(2,1)S(1)}, bf16[256,1152]{1,0:T(8,128)(2,1)S(1)}, u32[]{:S(2)}, u32[]{:S(2)}) collective-permute-start(bf16[256,1152]{1,0:T(8,128)(2,1)S(1)} %get-tuple-element.43), channel_id=1, source_target_pairs={{0,4},{4,0},{8,12},{12,8},{16,20},{20,16},{24,28},{28,24},{32,36},... | collective-permute-start | bytes 1769480 | tf_op jit(solution)/shard_map/ppermute | solution.py:23
  47.8 2.3 %collective-permute-start.8 = (bf16[272,1152]{1,0:T(8,128)(2,1)S(1)}, bf16[272,1152]{1,0:T(8,128)(2,1)S(1)}, u32[]{:S(2)}, u32[]{:S(2)}) collective-permute-start(bf16[272,1152]{1,0:T(8,128)(2,1)S(1)} %collective-permute-done.4.refs_1_), channel_id=1, source_target_pairs={{0,1},{1,0},{2,3},{3,2},{4,5},{5,4},{6,7},{7,6},{8,9},{9,8},{10,11... | collective-permute-start | bytes 1880072 | tf_op jit(solution)/shard_map/ppermute | solution.py:25
  53.6 5.3 %collective-permute-start.11 = (bf16[256,1152]{1,0:T(8,128)(2,1)S(1)}, bf16[256,1152]{1,0:T(8,128)(2,1)S(1)}, u32[]{:S(2)}, u32[]{:S(2)}) collective-permute-start(bf16[256,1152]{1,0:T(8,128)(2,1)S(1)} %get-tuple-element.48), channel_id=1, source_target_pairs={{0,1},{1,0},{2,3},{3,2},{4,5},{5,4},{6,7},{7,6},{8,9},{9,8},{10,11... | collective-permute-start | bytes 1769480 | tf_op jit(solution)/shard_map/ppermute | solution.py:25
  54.2 22.3 %collective-permute-start.14 = (bf16[256,1152]{1,0:T(8,128)(2,1)S(1)}, bf16[256,1152]{1,0:T(8,128)(2,1)S(1)}, u32[]{:S(2)}, u32[]{:S(2)}) collective-permute-start(bf16[256,1152]{1,0:T(8,128)(2,1)S(1)} %get-tuple-element.51), channel_id=1, source_target_pairs={{0,4},{4,0},{8,12},{12,8},{16,20},{20,16},{24,28},{28,24},{32,36},... | collective-permute-start | bytes 1769480 | tf_op jit(solution)/shard_map/ppermute | solution.py:23
  55.7 20.8 %collective-permute-start.15 = (bf16[256,1152]{1,0:T(8,128)(2,1)S(1)}, bf16[256,1152]{1,0:T(8,128)(2,1)S(1)}, u32[]{:S(2)}, u32[]{:S(2)}) collective-permute-start(bf16[256,1152]{1,0:T(8,128)(2,1)S(1)} %get-tuple-element.52), channel_id=1, source_target_pairs={{0,128},{4,132},{8,136},{12,140},{16,144},{20,148},{24,152},{28,15... | collective-permute-start | bytes 1769480 | tf_op jit(solution)/shard_map/ppermute | solution.py:23
  61.3 37.7 %collective-permute-start.22 = (bf16[256,1152]{1,0:T(8,128)(2,1)S(1)}, bf16[256,1152]{1,0:T(8,128)(2,1)S(1)}, u32[]{:S(2)}, u32[]{:S(2)}) collective-permute-start(bf16[256,1152]{1,0:T(8,128)(2,1)S(1)} %get-tuple-element.54), channel_id=1, source_target_pairs={{0,18},{1,19},{2,16},{3,17},{4,22},{5,23},{6,20},{7,21},{8,26},{9,... | collective-permute-start | bytes 1769480 | tf_op jit(solution)/shard_map/ppermute | solution.py:27
  61.5 7.1 %collective-permute-start.12 = (f32[8,128]{1,0:T(8,128)S(1)}, f32[8,128]{1,0:T(8,128)S(1)}, u32[]{:S(2)}, u32[]{:S(2)}) collective-permute-start(f32[8,128]{1,0:T(8,128)S(1)} %shard_map.90.refs_0_), channel_id=1, source_target_pairs={{0,16},{4,20},{8,24},{12,28},{16,0},{20,4},{24,8},{28,12},{32,48},... | collective-permute-start | bytes 12296 | tf_op jit(solution)/shard_map/ppermute | solution.py:23
  68.6 7.9 %collective-permute-start.13 = (f32[8,128]{1,0:T(8,128)S(1)}, f32[8,128]{1,0:T(8,128)S(1)}, u32[]{:S(2)}, u32[]{:S(2)}) collective-permute-start(f32[8,128]{1,0:T(8,128)S(1)} %shard_map.92.refs_0_), channel_id=1, source_target_pairs={{0,2},{1,3},{2,0},{3,1},{4,6},{5,7},{6,4},{7,5},{8,10},{9,11},{10,... | collective-permute-start | bytes 12296 | tf_op jit(solution)/shard_map/ppermute | solution.py:25
  76.7 2.4 %collective-permute-start.16 = (f32[8,128]{1,0:T(8,128)S(1)}, f32[8,128]{1,0:T(8,128)S(1)}, u32[]{:S(2)}, u32[]{:S(2)}) collective-permute-start(f32[8,128]{1,0:T(8,128)S(1)} %shard_map.94.refs_3_.refs_0_), channel_id=1, source_target_pairs={{0,1},{1,0},{2,3},{3,2},{4,5},{5,4},{6,7},{7,6},{8,9},{9,8},{10,11... | collective-permute-start | bytes 12296 | tf_op jit(solution)/shard_map/ppermute | solution.py:25
  76.8 27.7 %collective-permute-start.23 = (bf16[256,1152]{1,0:T(8,128)(2,1)S(1)}, bf16[256,1152]{1,0:T(8,128)(2,1)S(1)}, u32[]{:S(2)}, u32[]{:S(2)}) collective-permute-start(bf16[256,1152]{1,0:T(8,128)(2,1)S(1)} %shard_map.95), channel_id=1, source_target_pairs={{0,16},{4,20},{8,24},{12,28},{16,0},{20,4},{24,8},{28,12},{32,48},... | collective-permute-start | bytes 1769480 | tf_op jit(solution)/shard_map/ppermute | solution.py:23
  79.1 4.8 %collective-permute-start.17 = (f32[8,128]{1,0:T(8,128)S(1)}, f32[8,128]{1,0:T(8,128)S(1)}, u32[]{:S(2)}, u32[]{:S(2)}) collective-permute-start(f32[8,128]{1,0:T(8,128)S(1)} %shard_map.97.refs_0_), channel_id=1, source_target_pairs={{0,12},{4,8},{8,4},{12,0},{16,28},{20,24},{24,20},{28,16},{32,44},... | collective-permute-start | bytes 12296 | tf_op jit(solution)/shard_map/ppermute | solution.py:23
  83.9 5.1 %collective-permute-start.18 = (f32[8,128]{1,0:T(8,128)S(1)}, f32[8,128]{1,0:T(8,128)S(1)}, u32[]{:S(2)}, u32[]{:S(2)}) collective-permute-start(f32[8,128]{1,0:T(8,128)S(1)} %shard_map.99.refs_0_), channel_id=1, source_target_pairs={{0,8},{4,12},{8,0},{12,4},{16,24},{20,28},{24,16},{28,20},{32,40},... | collective-permute-start | bytes 12296 | tf_op jit(solution)/shard_map/ppermute | solution.py:23
  89.0 3.6 %collective-permute-start.19 = (f32[8,128]{1,0:T(8,128)S(1)}, f32[8,128]{1,0:T(8,128)S(1)}, u32[]{:S(2)}, u32[]{:S(2)}) collective-permute-start(f32[8,128]{1,0:T(8,128)S(1)} %shard_map.101.refs_0_), channel_id=1, source_target_pairs={{0,64},{4,68},{8,72},{12,76},{16,80},{20,84},{24,88},{28,92},{32,9... | collective-permute-start | bytes 12296 | tf_op jit(solution)/shard_map/ppermute | solution.py:23
  92.7 4.8 %collective-permute-start.20 = (f32[8,128]{1,0:T(8,128)S(1)}, f32[8,128]{1,0:T(8,128)S(1)}, u32[]{:S(2)}, u32[]{:S(2)}) collective-permute-start(f32[8,128]{1,0:T(8,128)S(1)} %shard_map.103.refs_0_), channel_id=1, source_target_pairs={{0,192},{4,196},{8,200},{12,204},{16,208},{20,212},{24,216},{28,22... | collective-permute-start | bytes 12296 | tf_op jit(solution)/shard_map/ppermute | solution.py:23
  97.5 6.3 %collective-permute-start.21 = (f32[8,128]{1,0:T(8,128)S(1)}, f32[8,128]{1,0:T(8,128)S(1)}, u32[]{:S(2)}, u32[]{:S(2)}) collective-permute-start(f32[8,128]{1,0:T(8,128)S(1)} %shard_map.105.refs_0_), channel_id=1, source_target_pairs={{0,32},{4,36},{8,40},{12,44},{16,48},{20,52},{24,56},{28,60},{32,0... | collective-permute-start | bytes 12296 | tf_op jit(solution)/shard_map/ppermute | solution.py:23
  (4 other events, 15.3 us)

commit v3 on v2

--- a/solution.py
+++ b/solution.py
@@ -287,75 +287,84 @@
 
     scalars = jnp.concatenate([jnp.exp(natural_odds_factor), bias])
     texts = caption_vectors
-    texts_z = exchange(texts, z_bit)
+    cut = rows // 4
+    texts_z0 = exchange(texts[:cut], z_bit)
+    texts_z1 = exchange(texts[cut:], z_bit)
+    texts_z = jnp.concatenate([texts_z0, texts_z1])
     texts_x = exchange(texts, x_bit)
     texts_y = exchange(texts, y_bit)
     (own,) = pack_weights(images, sample_weight, [(0, rows)])
     other = exchange(own, 0, core)
 
-    away = exchange(held_back(own, texts_z), z_bit, far)
+    (d0,), ((image_own,), (image_other,)), sums_a = pair_terms(
+        scalars, [[own], [other]], [[texts]], [f32], [[f32], [f32]], positive=True
+    )
+    away = exchange(held_back(own, texts_z0), z_bit, far)
     texts_zx = exchange(texts_z, x_bit)
     texts_zy = exchange(texts_z, y_bit)
-    (d0, dz, dx, dy), ((image_own,), (image_other,)), sums_a = pair_terms(
+    (dz, dx, dy), ((image_own,), (image_other,)), sums_b = pair_terms(
         scalars,
         [[own], [other]],
-        [[texts], [texts_z], [texts_x], [texts_y]],
-        [f32, f32, bf16, bf16],
+        [[texts_z], [texts_x], [texts_y]],
+        [f32, bf16, bf16],
         [[bf16], [bf16]],
-        positive=True,
+        add_image=[[image_own], [image_other]],
+        after=(sums_a,),
     )
     image_back = exchange(image_other, 0, core)
-    image_near = add_up(bf16, [image_own, image_back])
-
-    away = held_back(away, image_near, texts_zx, texts_zy)
+
+    away = held_back(away, sums_b)
     away_other = exchange(away, 0, core)
-    dx_back = exchange(held_back(dx, texts_zx), x_bit)
-    dy_back = exchange(held_back(dy, texts_zy), y_bit)
-    (dzx, dzy), (far_own,), sums_b = pair_terms(
+    (d0, dz), (far_own,), sums_c = pair_terms(
         scalars,
         [[away]],
-        [[texts_zx], [texts_zy]],
+        [[texts], [texts_z]],
         [f32, f32],
         [[f32]],
+        add_text=[[d0], [dz]],
         flops=LONG,
     )
-    (d0, dz, dzx, dzy), ((far_other,),), sums_c = pair_terms(
+    (d0, dz), (far_other,), sums_d = pair_terms(
         scalars,
         [[away_other]],
-        [[texts], [texts_z], [texts_zx], [texts_zy]],
-        [f32, f32, bf16, bf16],
-        [[bf16]],
-        add_text=[[d0], [dz], [dzx], [dzy]],
-        after=(sums_b,),
+        [[texts], [texts_z]],
+        [bf16, f32],
+        [[f32]],
+        add_text=[[d0], [dz]],
+        after=(sums_c,),
+    )
+    (dzx, dzy), ((far_own,), (far_other,)), sums_e = pair_terms(
+        scalars,
+        [[away], [away_other]],
+        [[texts_zx], [texts_zy]],
+        [bf16, bf16],
+        [[f32], [bf16]],
+        add_image=[far_own, far_other],
+        after=(sums_d,),
     )
     near_back = exchange(far_other, 0, core)
     dzx_back = exchange(dzx, x_bit)
     dzy_back = exchange(dzy, y_bit)
-    (d0, dz), ((far_total,),), sums_d = pair_terms(
-        scalars,
-        [[away]],
-        [[texts], [texts_z]],
-        [bf16, f32],
-        [[bf16]],
-        add_text=[[d0, dx_back, dy_back], [dz]],
-        add_image=[[*far_own, near_back]],
-        after=(sums_c,),
-    )
+    far_total = add_up(bf16, [far_own, near_back], (beside(sums_e),))
     image_away = exchange(far_total, z_bit, far)
-
-    sums = add_up(f32, [sums_a, sums_b, sums_c, sums_d])
+    image_near = add_up(bf16, [image_own, image_back], (far_total,))
+
+    sums = add_up(f32, [sums_a, sums_b, sums_c, sums_d, sums_e], (far_total, image_near))
     sums = all_sum_step(sums, z_bit, 0)
     sums = all_sum_step(sums, 0, far)
     dz_total = add_up(bf16, [dz, dzx_back, dzy_back], (sums,))
     dz_back = exchange(dz_total, z_bit)
+    dx_back = exchange(held_back(dx, far_total), x_bit)
+    dy_back = exchange(held_back(dy, far_total), y_bit)
     sums = all_sum_step(held_back(sums, dz_total), 0, core)
     sums = all_sum_step(sums, 3 * x_bit, 0)
     sums = all_sum_step(sums, 2 * x_bit, 0)
     sums = all_sum_step(sums, y_bit // 2, 0)
     sums = all_sum_step(sums, y_bit // 2 * 3, 0)
     received = exchange(sums, 2 * z_bit)
+    d0 = add_up(bf16, [d0, dx_back, dy_back])
     grad_images = (image_near.astype(f32) + image_away).astype(bf16)
-    sums = add_up(f32, [sums, received], (grad_images,))
+    sums = add_up(f32, [sums, received], (grad_images, d0))
     totals = jnp.sum(sums, axis=1)
 
     pair_count = float(rows * rep_count * groups * rows * rep_count * (ROUNDS + 1))

time: 108 us -> 105 us (0.972)
  starting transfers between devices: 41.4 us -> 38.1 us
  Pallas kernels: 15.1 us -> 16.3 us
    ppermute x16 -> x17, starting transfers between devices: 34.1 us -> 24.6 us  [exchange(): lax.ppermute(value, 'batch', [(s, s ^ batch_mask) for s in range(batch)])]
    ppermute x2, starting transfers between devices: 4.86 us -> 12.5 us  [exchange(): lax.ppermute(value, ('batch', 'rep'), [(s, s ^ mask) for s in range(batch...]
    ppermute x2, waiting for transfers between devices: 6.59 us -> 0.01 us  [exchange(): lax.ppermute(value, ('batch', 'rep'), [(s, s ^ mask) for s in range(batch...]
    ppermute x16 -> x17, waiting for transfers between devices: 30.3 us -> 34.9 us  [exchange(): lax.ppermute(value, 'batch', [(s, s ^ batch_mask) for s in range(batch)])]
    slice x0 -> x2, local copies, waits for them, and re-layouts: none -> 2.06 us  [the longest x1 1.05 us: on_device(): texts_z1 = exchange(texts[cut:], z_bit)]
    unnamed x8 -> x9, local copies, waits for them, and re-layouts: 1.75 us -> 0.03 us
    ppermute x6, starting transfers between devices: 2.45 us -> 0.99 us  [exchange(): return lax.ppermute(value, 'rep', [(s, s ^ rep_mask) for s in range(rep)])]
    ppermute x6, waiting for transfers between devices: 6.3 us -> 7.48 us  [exchange(): return lax.ppermute(value, 'rep', [(s, s ^ rep_mask) for s in range(rep)])]
  transfers between devices with their start and end apart: 24 -> 25, of which waited for: 10 -> 11; matrix products, arithmetic and copies ran while one was open for 1% -> 2% of each run, Pallas kernels for 14% -> 16%
where the time goes in v3:
time: 105 us; the launch traced here: 104 us
  waiting for transfers between devices  42.4 us (40%)
  starting transfers between devices  38.1 us (36%)
  Pallas kernels  16.3 us (16%)
  between operations  3.4 us (3%)
  local copies, waits for them, and re-layouts  2.14 us (2%)
  other arithmetic  1.92 us (2%)
    ppermute x17, waiting for transfers between devices, exchange(): lax.ppermute(value, 'batch', [(s, s ^ batch_mask) for s in range(batch)])  34.9 us
    ppermute x17, starting transfers between devices, exchange(): lax.ppermute(value, 'batch', [(s, s ^ batch_mask) for s in range(batch)])  24.6 us
    pallas_call x5, Pallas kernels, pair_terms(): pl.pallas_call(functools.partial(pair_kernel, [len(pieces) for pieces in...  15.4 us
    ppermute x2, starting transfers between devices, exchange(): lax.ppermute(value, ('batch', 'rep'), [(s, s ^ mask) for s in range(batch...  12.5 us
    ppermute x6, waiting for transfers between devices, exchange(): return lax.ppermute(value, 'rep', [(s, s ^ rep_mask) for s in range(rep)])  7.48 us
  transfers between devices with their start and end apart: 25, of which 11 were waited for; matrix products, arithmetic and copies ran while one was open for 2% of the time, Pallas kernels for 16%

profile of v3, /device:TPU:64, one launch (start us, length us, event | category | flops | bytes accessed | tf_op | source)
XLA Modules:
  0.0 104.2 jit_solution(13939219441471710895)
XLA Ops:
  1.7 2.0 %collective-permute-start.1 = (bf16[64,1152]{1,0:T(8,128)(2,1)S(1)}, bf16[64,1152]{1,0:T(8,128)(2,1)S(1)}, u32[]{:S(2)}, u32[]{:S(2)}) collective-permute-start(bf16[64,1152]{1,0:T(8,128)(2,1)S(1)} %slice.12), channel_id=1, source_target_pairs={{0,16},{4,20},{8,24},{12,28},{16,0},{20,4},{24,8},{28,12},{32,48},... | collective-permute-start | bytes 442376 | tf_op jit(solution)/shard_map/ppermute | solution.py:23
  5.2 2.8 %collective-permute-done.1 = bf16[64,1152]{1,0:T(8,128)(2,1)S(1)} collective-permute-done((bf16[64,1152]{1,0:T(8,128)(2,1)S(1)}, bf16[64,1152]{1,0:T(8,128)(2,1)S(1)}, u32[]{:S(2)}, u32[]{:S(2)}) %collective-permute-start.1) | collective-permute-done | bytes 147488 | tf_op jit(solution)/shard_map/ppermute | solution.py:23
  8.0 5.4 %collective-permute-start.5 = (bf16[272,1152]{1,0:T(8,128)(2,1)S(1)}, bf16[272,1152]{1,0:T(8,128)(2,1)S(1)}, u32[]{:S(2)}, u32[]{:S(2)}) collective-permute-start(bf16[272,1152]{1,0:T(8,128)(2,1)S(1)} %shard_map.84.refs_1_), channel_id=1, source_target_pairs={{0,18},{1,19},{2,16},{3,17},{4,22},{5,23},{6,20},{7,21},{8,26},{9,... | collective-permute-start | bytes 1880072 | tf_op jit(solution)/shard_map/ppermute | solution.py:27
  14.9 3.2 %collective-permute-start.4 = (bf16[256,1152]{1,0:T(8,128)(2,1)S(1)}, bf16[256,1152]{1,0:T(8,128)(2,1)S(1)}, u32[]{:S(2)}, u32[]{:S(2)}) collective-permute-start(bf16[256,1152]{1,0:T(8,128)(2,1)S(1)} %copy-done), channel_id=1, source_target_pairs={{0,128},{4,132},{8,136},{12,140},{16,144},{20,148},{24,152},{28,15... | collective-permute-start | bytes 1769480 | tf_op jit(solution)/shard_map/ppermute | solution.py:23
  19.6 7.7 %collective-permute-done.2 = bf16[192,1152]{1,0:T(8,128)(2,1)S(1)} collective-permute-done((bf16[192,1152]{1,0:T(8,128)(2,1)S(1)}, bf16[192,1152]{1,0:T(8,128)(2,1)S(1)}, u32[]{:S(2)}, u32[]{:S(2)}) %collective-permute-start.2) | collective-permute-done | bytes 442400 | tf_op jit(solution)/shard_map/ppermute | solution.py:23
  27.3 1.6 %collective-permute-start.7 = (bf16[256,1152]{1,0:T(8,128)(2,1)S(1)}, bf16[256,1152]{1,0:T(8,128)(2,1)S(1)}, u32[]{:S(2)}, u32[]{:S(2)}) collective-permute-start(bf16[256,1152]{1,0:T(8,128)(2,1)S(1)} %constant_dynamic-update-slice_fusion.refs_3_), channel_id=1, source_target_pairs={{0,4},{4,0},{8,12},{12,8},{16,20},{20,16},{24,28},{28,24},{32,36},... | collective-permute-start | bytes 1769480 | tf_op jit(solution)/shard_map/ppermute | solution.py:23
  28.9 3.2 %collective-permute-start.8 = (bf16[256,1152]{1,0:T(8,128)(2,1)S(1)}, bf16[256,1152]{1,0:T(8,128)(2,1)S(1)}, u32[]{:S(2)}, u32[]{:S(2)}) collective-permute-start(bf16[256,1152]{1,0:T(8,128)(2,1)S(1)} %constant_dynamic-update-slice_fusion.refs_3_), channel_id=1, source_target_pairs={{0,128},{4,132},{8,136},{12,140},{16,144},{20,148},{24,152},{28,15... | collective-permute-start | bytes 1769480 | tf_op jit(solution)/shard_map/ppermute | solution.py:23
  32.1 2.3 %shard_map.85 = (f32[256,1152]{1,0:T(8,128)S(1)}, f32[256,1152]{1,0:T(8,128)S(1)}, f32[256,1152]{1,0:T(8,128)S(1)}, f32[8,128]{1,0:T(8,128)S(1)}) custom-call(f32[2]{0:T(128)S(1)} %pad_maximum_fusion.refs_0_, bf16[272,1152]{1,0:T(8,128)(2,1)S(1)} %shard_map.84.refs_1_, bf16[272,1152]{1,0:T(8,128)(2,1)S(1)} %collective-permute-done.refs_2_, ...), custom_call_target="tpu_custom_call" | custom-call | flops 1 | bytes 1 | tf_op jit(solution)/shard_map/pallas_call | solution.py:246
  34.5 4.9 %shard_map.86 = (f32[256,1152]{1,0:T(8,128)S(1)}, bf16[256,1152]{1,0:T(8,128)(2,1)S(1)}, bf16[256,1152]{1,0:T(8,128)(2,1)S(1)}, bf16[256,1152]{1,0:T(8,128)(2,1)...) custom-call(f32[2]{0:T(128)S(1)} %pad_maximum_fusion.refs_0_, bf16[272,1152]{1,0:T(8,128)(2,1)S(1)} %shard_map.84.refs_1_, ...), custom_call_target="tpu_custom_call" | custom-call | flops 1 | bytes 1 | tf_op jit(solution)/shard_map/pallas_call | solution.py:246
  39.9 2.3 %shard_map.87 = (f32[256,1152]{1,0:T(8,128)S(1)}, f32[256,1152]{1,0:T(8,128)S(1)}, f32[256,1152]{1,0:T(8,128)S(1)}, f32[8,128]{1,0:T(8,128)S(1)}) custom-call(f32[2]{0:T(128)S(1)} %pad_maximum_fusion.refs_0_, bf16[272,1152]{1,0:T(8,128)(2,1)S(1)} %collective-permute-done.5.refs_1_, bf16[256,1152]{1,0:T(8,128)(2,1)S(1)} %copy-done, ...), custom_call_target="tpu_custom_call" | custom-call | flops 10000000000 | bytes 1 | tf_op jit(solution)/shard_map/pallas_call | solution.py:246
  42.3 2.3 %shard_map.88 = (bf16[256,1152]{1,0:T(8,128)(2,1)S(1)}, f32[256,1152]{1,0:T(8,128)S(1)}, f32[256,1152]{1,0:T(8,128)S(1)}, f32[8,128]{1,0:T(8,128)S(1)}) custom-call(f32[2]{0:T(128)S(1)} %pad_maximum_fusion.refs_0_, bf16[272,1152]{1,0:T(8,128)(2,1)S(1)} %collective-permute-done.6.refs_1_.refs_2_, bf16[256,1152]{1,0:T(8,128)(2,1)S(1)} %copy-done, ...), custom_call_target="tpu_custom_call" | custom-call | flops 1 | bytes 1 | tf_op jit(solution)/shard_map/pallas_call | solution.py:246
  44.6 3.6 %shard_map.89 = (bf16[256,1152]{1,0:T(8,128)(2,1)S(1)}, bf16[256,1152]{1,0:T(8,128)(2,1)S(1)}, f32[256,1152]{1,0:T(8,128)S(1)}, bf16[256,1152]{1,0:T(8,128)(2,1)S(1)}, f32[8,128]{1,0:T(8,128)S(1)}) custom-call(f32[2]{0:T(128)S(1)} %pad_maximum_fusion.refs_0_, bf16[272,1152]{1,0:T(8,128)(2,1)S(1)} %collective-permute-done.5.refs_1_, ...), custom_call_target="tpu_custom_call" | custom-call | flops 1 | bytes 1 | tf_op jit(solution)/shard_map/pallas_call | solution.py:246
  49.6 3.2 %collective-permute-start.14 = (bf16[256,1152]{1,0:T(8,128)(2,1)S(1)}, bf16[256,1152]{1,0:T(8,128)(2,1)S(1)}, u32[]{:S(2)}, u32[]{:S(2)}) collective-permute-start(bf16[256,1152]{1,0:T(8,128)(2,1)S(1)} %get-tuple-element.53), channel_id=1, source_target_pairs={{0,128},{4,132},{8,136},{12,140},{16,144},{20,148},{24,152},{28,15... | collective-permute-start | bytes 1769480 | tf_op jit(solution)/shard_map/ppermute | solution.py:23
  52.9 7.1 %collective-permute-start.21 = (bf16[256,1152]{1,0:T(8,128)(2,1)S(1)}, bf16[256,1152]{1,0:T(8,128)(2,1)S(1)}, u32[]{:S(2)}, u32[]{:S(2)}) collective-permute-start(bf16[256,1152]{1,0:T(8,128)(2,1)S(1)} %shard_map.91.refs_2_.refs_5_), channel_id=1, source_target_pairs={{0,18},{1,19},{2,16},{3,17},{4,22},{5,23},{6,20},{7,21},{8,26},{9,... | collective-permute-start | bytes 1769480 | tf_op jit(solution)/shard_map/ppermute | solution.py:27
  60.3 3.9 %collective-permute-done.11.refs_1_ = f32[8,128]{1,0:T(8,128)S(1)} collective-permute-done((f32[8,128]{1,0:T(8,128)S(1)}, f32[8,128]{1,0:T(8,128)S(1)}, u32[]{:S(2)}, u32[]{:S(2)}) %collective-permute-start.11) | collective-permute-done | bytes 4128 | tf_op jit(solution)/shard_map/ppermute | solution.py:23
  65.6 6.2 %collective-permute-done.12.refs_1_ = f32[8,128]{1,0:T(8,128)S(1)} collective-permute-done((f32[8,128]{1,0:T(8,128)S(1)}, f32[8,128]{1,0:T(8,128)S(1)}, u32[]{:S(2)}, u32[]{:S(2)}) %collective-permute-start.12) | collective-permute-done | bytes 4128 | tf_op jit(solution)/shard_map/ppermute | solution.py:25
  71.8 1.5 %collective-permute-start.22 = (bf16[256,1152]{1,0:T(8,128)(2,1)S(1)}, bf16[256,1152]{1,0:T(8,128)(2,1)S(1)}, u32[]{:S(2)}, u32[]{:S(2)}) collective-permute-start(bf16[256,1152]{1,0:T(8,128)(2,1)S(1)} %get-tuple-element.57), channel_id=1, source_target_pairs={{0,4},{4,0},{8,12},{12,8},{16,20},{20,16},{24,28},{28,24},{32,36},... | collective-permute-start | bytes 1769480 | tf_op jit(solution)/shard_map/ppermute | solution.py:23
  73.6 2.9 %collective-permute-start.24 = (bf16[256,1152]{1,0:T(8,128)(2,1)S(1)}, bf16[256,1152]{1,0:T(8,128)(2,1)S(1)}, u32[]{:S(2)}, u32[]{:S(2)}) collective-permute-start(bf16[256,1152]{1,0:T(8,128)(2,1)S(1)} %shard_map.98), channel_id=1, source_target_pairs={{0,16},{4,20},{8,24},{12,28},{16,0},{20,4},{24,8},{28,12},{32,48},... | collective-permute-start | bytes 1769480 | tf_op jit(solution)/shard_map/ppermute | solution.py:23
  77.7 4.8 %collective-permute-done.16.refs_1_ = f32[8,128]{1,0:T(8,128)S(1)} collective-permute-done((f32[8,128]{1,0:T(8,128)S(1)}, f32[8,128]{1,0:T(8,128)S(1)}, u32[]{:S(2)}, u32[]{:S(2)}) %collective-permute-start.16) | collective-permute-done | bytes 4128 | tf_op jit(solution)/shard_map/ppermute | solution.py:23
  82.5 5.9 %collective-permute-done.17.refs_1_ = f32[8,128]{1,0:T(8,128)S(1)} collective-permute-done((f32[8,128]{1,0:T(8,128)S(1)}, f32[8,128]{1,0:T(8,128)S(1)}, u32[]{:S(2)}, u32[]{:S(2)}) %collective-permute-start.17) | collective-permute-done | bytes 4128 | tf_op jit(solution)/shard_map/ppermute | solution.py:23
  89.1 2.9 %collective-permute-done.18.refs_1_ = f32[8,128]{1,0:T(8,128)S(1)} collective-permute-done((f32[8,128]{1,0:T(8,128)S(1)}, f32[8,128]{1,0:T(8,128)S(1)}, u32[]{:S(2)}, u32[]{:S(2)}) %collective-permute-start.18) | collective-permute-done | bytes 4128 | tf_op jit(solution)/shard_map/ppermute | solution.py:23
  92.0 2.1 %collective-permute-start.19 = (f32[8,128]{1,0:T(8,128)S(1)}, f32[8,128]{1,0:T(8,128)S(1)}, u32[]{:S(2)}, u32[]{:S(2)}) collective-permute-start(f32[8,128]{1,0:T(8,128)S(1)} %shard_map.106.refs_0_), channel_id=1, source_target_pairs={{0,192},{4,196},{8,200},{12,204},{16,208},{20,212},{24,216},{28,22... | collective-permute-start | bytes 12296 | tf_op jit(solution)/shard_map/ppermute | solution.py:23
  94.2 2.7 %collective-permute-done.19.refs_1_ = f32[8,128]{1,0:T(8,128)S(1)} collective-permute-done((f32[8,128]{1,0:T(8,128)S(1)}, f32[8,128]{1,0:T(8,128)S(1)}, u32[]{:S(2)}, u32[]{:S(2)}) %collective-permute-start.19) | collective-permute-done | bytes 4128 | tf_op jit(solution)/shard_map/ppermute | solution.py:23
  97.3 4.1 %collective-permute-done.20.refs_1_ = f32[8,128]{1,0:T(8,128)S(1)} collective-permute-done((f32[8,128]{1,0:T(8,128)S(1)}, f32[8,128]{1,0:T(8,128)S(1)}, u32[]{:S(2)}, u32[]{:S(2)}) %collective-permute-start.20) | collective-permute-done | bytes 4128 | tf_op jit(solution)/shard_map/ppermute | solution.py:23
  (70 shorter events, 12.1 us)
Async XLA Ops:
  1.7 6.3 %collective-permute-start.1 = (bf16[64,1152]{1,0:T(8,128)(2,1)S(1)}, bf16[64,1152]{1,0:T(8,128)(2,1)S(1)}, u32[]{:S(2)}, u32[]{:S(2)}) collective-permute-start(bf16[64,1152]{1,0:T(8,128)(2,1)S(1)} %slice.12), channel_id=1, source_target_pairs={{0,16},{4,20},{8,24},{12,28},{16,0},{20,4},{24,8},{28,12},{32,48},... | collective-permute-start | bytes 442376 | tf_op jit(solution)/shard_map/ppermute | solution.py:23
  4.7 22.5 %collective-permute-start.2 = (bf16[192,1152]{1,0:T(8,128)(2,1)S(1)}, bf16[192,1152]{1,0:T(8,128)(2,1)S(1)}, u32[]{:S(2)}, u32[]{:S(2)}) collective-permute-start(bf16[192,1152]{1,0:T(8,128)(2,1)S(1)} %slice.13), channel_id=1, source_target_pairs={{0,16},{4,20},{8,24},{12,28},{16,0},{20,4},{24,8},{28,12},{32,48},... | collective-permute-start | bytes 1327112 | tf_op jit(solution)/shard_map/ppermute | solution.py:23
  5.1 23.8 %collective-permute-start = (bf16[272,1152]{1,0:T(8,128)(2,1)S(1)}, bf16[272,1152]{1,0:T(8,128)(2,1)S(1)}, u32[]{:S(2)}, u32[]{:S(2)}) collective-permute-start(bf16[272,1152]{1,0:T(8,128)(2,1)S(1)} %shard_map.84.refs_1_), channel_id=1, source_target_pairs={{0,1},{1,0},{2,3},{3,2},{4,5},{5,4},{6,7},{7,6},{8,9},{9,8},{10,11... | collective-permute-start | bytes 1880072 | tf_op jit(solution)/shard_map/ppermute | solution.py:25
  8.0 31.4 %collective-permute-start.5 = (bf16[272,1152]{1,0:T(8,128)(2,1)S(1)}, bf16[272,1152]{1,0:T(8,128)(2,1)S(1)}, u32[]{:S(2)}, u32[]{:S(2)}) collective-permute-start(bf16[272,1152]{1,0:T(8,128)(2,1)S(1)} %shard_map.84.refs_1_), channel_id=1, source_target_pairs={{0,18},{1,19},{2,16},{3,17},{4,22},{5,23},{6,20},{7,21},{8,26},{9,... | collective-permute-start | bytes 1880072 | tf_op jit(solution)/shard_map/ppermute | solution.py:27
  13.4 21.0 %collective-permute-start.3 = (bf16[256,1152]{1,0:T(8,128)(2,1)S(1)}, bf16[256,1152]{1,0:T(8,128)(2,1)S(1)}, u32[]{:S(2)}, u32[]{:S(2)}) collective-permute-start(bf16[256,1152]{1,0:T(8,128)(2,1)S(1)} %copy-done), channel_id=1, source_target_pairs={{0,4},{4,0},{8,12},{12,8},{16,20},{20,16},{24,28},{28,24},{32,36},... | collective-permute-start | bytes 1769480 | tf_op jit(solution)/shard_map/ppermute | solution.py:23
  14.9 19.5 %collective-permute-start.4 = (bf16[256,1152]{1,0:T(8,128)(2,1)S(1)}, bf16[256,1152]{1,0:T(8,128)(2,1)S(1)}, u32[]{:S(2)}, u32[]{:S(2)}) collective-permute-start(bf16[256,1152]{1,0:T(8,128)(2,1)S(1)} %copy-done), channel_id=1, source_target_pairs={{0,128},{4,132},{8,136},{12,140},{16,144},{20,148},{24,152},{28,15... | collective-permute-start | bytes 1769480 | tf_op jit(solution)/shard_map/ppermute | solution.py:23
  27.3 17.3 %collective-permute-start.7 = (bf16[256,1152]{1,0:T(8,128)(2,1)S(1)}, bf16[256,1152]{1,0:T(8,128)(2,1)S(1)}, u32[]{:S(2)}, u32[]{:S(2)}) collective-permute-start(bf16[256,1152]{1,0:T(8,128)(2,1)S(1)} %constant_dynamic-update-slice_fusion.refs_3_), channel_id=1, source_target_pairs={{0,4},{4,0},{8,12},{12,8},{16,20},{20,16},{24,28},{28,24},{32,36},... | collective-permute-start | bytes 1769480 | tf_op jit(solution)/shard_map/ppermute | solution.py:23
  28.9 15.7 %collective-permute-start.8 = (bf16[256,1152]{1,0:T(8,128)(2,1)S(1)}, bf16[256,1152]{1,0:T(8,128)(2,1)S(1)}, u32[]{:S(2)}, u32[]{:S(2)}) collective-permute-start(bf16[256,1152]{1,0:T(8,128)(2,1)S(1)} %constant_dynamic-update-slice_fusion.refs_3_), channel_id=1, source_target_pairs={{0,128},{4,132},{8,136},{12,140},{16,144},{20,148},{24,152},{28,15... | collective-permute-start | bytes 1769480 | tf_op jit(solution)/shard_map/ppermute | solution.py:23
  39.3 20.7 %collective-permute-start.10 = (bf16[256,1152]{1,0:T(8,128)(2,1)S(1)}, bf16[256,1152]{1,0:T(8,128)(2,1)S(1)}, u32[]{:S(2)}, u32[]{:S(2)}) collective-permute-start(bf16[256,1152]{1,0:T(8,128)(2,1)S(1)} %get-tuple-element.50), channel_id=1, source_target_pairs={{0,1},{1,0},{2,3},{3,2},{4,5},{5,4},{6,7},{7,6},{8,9},{9,8},{10,11... | collective-permute-start | bytes 1769480 | tf_op jit(solution)/shard_map/ppermute | solution.py:25
  39.4 2.9 %collective-permute-start.6 = (bf16[272,1152]{1,0:T(8,128)(2,1)S(1)}, bf16[272,1152]{1,0:T(8,128)(2,1)S(1)}, u32[]{:S(2)}, u32[]{:S(2)}) collective-permute-start(bf16[272,1152]{1,0:T(8,128)(2,1)S(1)} %collective-permute-done.5.refs_1_), channel_id=1, source_target_pairs={{0,1},{1,0},{2,3},{3,2},{4,5},{5,4},{6,7},{7,6},{8,9},{9,8},{10,11... | collective-permute-start | bytes 1880072 | tf_op jit(solution)/shard_map/ppermute | solution.py:25
  48.2 4.5 %collective-permute-start.9 = (bf16[256,1152]{1,0:T(8,128)(2,1)S(1)}, bf16[256,1152]{1,0:T(8,128)(2,1)S(1)}, u32[]{:S(2)}, u32[]{:S(2)}) collective-permute-start(bf16[256,1152]{1,0:T(8,128)(2,1)S(1)} %get-tuple-element.48), channel_id=1, source_target_pairs={{0,1},{1,0},{2,3},{3,2},{4,5},{5,4},{6,7},{7,6},{8,9},{9,8},{10,11... | collective-permute-start | bytes 1769480 | tf_op jit(solution)/shard_map/ppermute | solution.py:25
  48.5 24.8 %collective-permute-start.13 = (bf16[256,1152]{1,0:T(8,128)(2,1)S(1)}, bf16[256,1152]{1,0:T(8,128)(2,1)S(1)}, u32[]{:S(2)}, u32[]{:S(2)}) collective-permute-start(bf16[256,1152]{1,0:T(8,128)(2,1)S(1)} %get-tuple-element.52), channel_id=1, source_target_pairs={{0,4},{4,0},{8,12},{12,8},{16,20},{20,16},{24,28},{28,24},{32,36},... | collective-permute-start | bytes 1769480 | tf_op jit(solution)/shard_map/ppermute | solution.py:23
  49.6 23.8 %collective-permute-start.14 = (bf16[256,1152]{1,0:T(8,128)(2,1)S(1)}, bf16[256,1152]{1,0:T(8,128)(2,1)S(1)}, u32[]{:S(2)}, u32[]{:S(2)}) collective-permute-start(bf16[256,1152]{1,0:T(8,128)(2,1)S(1)} %get-tuple-element.53), channel_id=1, source_target_pairs={{0,128},{4,132},{8,136},{12,140},{16,144},{20,148},{24,152},{28,15... | collective-permute-start | bytes 1769480 | tf_op jit(solution)/shard_map/ppermute | solution.py:23
  52.9 43.9 %collective-permute-start.21 = (bf16[256,1152]{1,0:T(8,128)(2,1)S(1)}, bf16[256,1152]{1,0:T(8,128)(2,1)S(1)}, u32[]{:S(2)}, u32[]{:S(2)}) collective-permute-start(bf16[256,1152]{1,0:T(8,128)(2,1)S(1)} %shard_map.91.refs_2_.refs_5_), channel_id=1, source_target_pairs={{0,18},{1,19},{2,16},{3,17},{4,22},{5,23},{6,20},{7,21},{8,26},{9,... | collective-permute-start | bytes 1769480 | tf_op jit(solution)/shard_map/ppermute | solution.py:27
  60.2 4.0 %collective-permute-start.11 = (f32[8,128]{1,0:T(8,128)S(1)}, f32[8,128]{1,0:T(8,128)S(1)}, u32[]{:S(2)}, u32[]{:S(2)}) collective-permute-start(f32[8,128]{1,0:T(8,128)S(1)} %shard_map.93.refs_0_), channel_id=1, source_target_pairs={{0,16},{4,20},{8,24},{12,28},{16,0},{20,4},{24,8},{28,12},{32,48},... | collective-permute-start | bytes 12296 | tf_op jit(solution)/shard_map/ppermute | solution.py:23
  64.2 7.6 %collective-permute-start.12 = (f32[8,128]{1,0:T(8,128)S(1)}, f32[8,128]{1,0:T(8,128)S(1)}, u32[]{:S(2)}, u32[]{:S(2)}) collective-permute-start(f32[8,128]{1,0:T(8,128)S(1)} %shard_map.95.refs_0_), channel_id=1, source_target_pairs={{0,2},{1,3},{2,0},{3,1},{4,6},{5,7},{6,4},{7,5},{8,10},{9,11},{10,... | collective-permute-start | bytes 12296 | tf_op jit(solution)/shard_map/ppermute | solution.py:25
  64.2 32.9 %collective-permute-start.23 = (bf16[256,1152]{1,0:T(8,128)(2,1)S(1)}, bf16[256,1152]{1,0:T(8,128)(2,1)S(1)}, u32[]{:S(2)}, u32[]{:S(2)}) collective-permute-start(bf16[256,1152]{1,0:T(8,128)(2,1)S(1)} %get-tuple-element.59), channel_id=1, source_target_pairs={{0,128},{4,132},{8,136},{12,140},{16,144},{20,148},{24,152},{28,15... | collective-permute-start | bytes 1769480 | tf_op jit(solution)/shard_map/ppermute | solution.py:23
  71.8 25.2 %collective-permute-start.22 = (bf16[256,1152]{1,0:T(8,128)(2,1)S(1)}, bf16[256,1152]{1,0:T(8,128)(2,1)S(1)}, u32[]{:S(2)}, u32[]{:S(2)}) collective-permute-start(bf16[256,1152]{1,0:T(8,128)(2,1)S(1)} %get-tuple-element.57), channel_id=1, source_target_pairs={{0,4},{4,0},{8,12},{12,8},{16,20},{20,16},{24,28},{28,24},{32,36},... | collective-permute-start | bytes 1769480 | tf_op jit(solution)/shard_map/ppermute | solution.py:23
  73.6 28.6 %collective-permute-start.24 = (bf16[256,1152]{1,0:T(8,128)(2,1)S(1)}, bf16[256,1152]{1,0:T(8,128)(2,1)S(1)}, u32[]{:S(2)}, u32[]{:S(2)}) collective-permute-start(bf16[256,1152]{1,0:T(8,128)(2,1)S(1)} %shard_map.98), channel_id=1, source_target_pairs={{0,16},{4,20},{8,24},{12,28},{16,0},{20,4},{24,8},{28,12},{32,48},... | collective-permute-start | bytes 1769480 | tf_op jit(solution)/shard_map/ppermute | solution.py:23
  77.7 4.8 %collective-permute-start.16 = (f32[8,128]{1,0:T(8,128)S(1)}, f32[8,128]{1,0:T(8,128)S(1)}, u32[]{:S(2)}, u32[]{:S(2)}) collective-permute-start(f32[8,128]{1,0:T(8,128)S(1)} %shard_map.100.refs_0_), channel_id=1, source_target_pairs={{0,12},{4,8},{8,4},{12,0},{16,28},{20,24},{24,20},{28,16},{32,44},... | collective-permute-start | bytes 12296 | tf_op jit(solution)/shard_map/ppermute | solution.py:23
  82.5 5.9 %collective-permute-start.17 = (f32[8,128]{1,0:T(8,128)S(1)}, f32[8,128]{1,0:T(8,128)S(1)}, u32[]{:S(2)}, u32[]{:S(2)}) collective-permute-start(f32[8,128]{1,0:T(8,128)S(1)} %shard_map.102.refs_0_), channel_id=1, source_target_pairs={{0,8},{4,12},{8,0},{12,4},{16,24},{20,28},{24,16},{28,20},{32,40},... | collective-permute-start | bytes 12296 | tf_op jit(solution)/shard_map/ppermute | solution.py:23
  88.4 3.6 %collective-permute-start.18 = (f32[8,128]{1,0:T(8,128)S(1)}, f32[8,128]{1,0:T(8,128)S(1)}, u32[]{:S(2)}, u32[]{:S(2)}) collective-permute-start(f32[8,128]{1,0:T(8,128)S(1)} %shard_map.104.refs_0_), channel_id=1, source_target_pairs={{0,64},{4,68},{8,72},{12,76},{16,80},{20,84},{24,88},{28,92},{32,9... | collective-permute-start | bytes 12296 | tf_op jit(solution)/shard_map/ppermute | solution.py:23
  92.0 4.8 %collective-permute-start.19 = (f32[8,128]{1,0:T(8,128)S(1)}, f32[8,128]{1,0:T(8,128)S(1)}, u32[]{:S(2)}, u32[]{:S(2)}) collective-permute-start(f32[8,128]{1,0:T(8,128)S(1)} %shard_map.106.refs_0_), channel_id=1, source_target_pairs={{0,192},{4,196},{8,200},{12,204},{16,208},{20,212},{24,216},{28,22... | collective-permute-start | bytes 12296 | tf_op jit(solution)/shard_map/ppermute | solution.py:23
  96.9 4.5 %collective-permute-start.20 = (f32[8,128]{1,0:T(8,128)S(1)}, f32[8,128]{1,0:T(8,128)S(1)}, u32[]{:S(2)}, u32[]{:S(2)}) collective-permute-start(f32[8,128]{1,0:T(8,128)S(1)} %shard_map.108.refs_0_), channel_id=1, source_target_pairs={{0,32},{4,36},{8,40},{12,44},{16,48},{20,52},{24,56},{28,60},{32,0... | collective-permute-start | bytes 12296 | tf_op jit(solution)/shard_map/ppermute | solution.py:23
  (5 other events, 26.9 us)

commit v4 on v3

--- a/solution.py
+++ b/solution.py
@@ -342,22 +342,24 @@
         add_image=[far_own, far_other],
         after=(sums_d,),
     )
+    sums = add_up(f32, [sums_a, sums_b, sums_c, sums_d, sums_e])
+    received = exchange(sums, 0, core)
     near_back = exchange(far_other, 0, core)
     dzx_back = exchange(dzx, x_bit)
     dzy_back = exchange(dzy, y_bit)
-    far_total = add_up(bf16, [far_own, near_back], (beside(sums_e),))
+    mark = beside(sums_e)
+    sums = add_up(f32, [sums, received], (mark,))
+    far_total = add_up(bf16, [far_own, near_back], (mark, sums))
     image_away = exchange(far_total, z_bit, far)
     image_near = add_up(bf16, [image_own, image_back], (far_total,))
 
-    sums = add_up(f32, [sums_a, sums_b, sums_c, sums_d, sums_e], (far_total, image_near))
-    sums = all_sum_step(sums, z_bit, 0)
+    sums = all_sum_step(held_back(sums, far_total), z_bit, 0)
     sums = all_sum_step(sums, 0, far)
     dz_total = add_up(bf16, [dz, dzx_back, dzy_back], (sums,))
     dz_back = exchange(dz_total, z_bit)
     dx_back = exchange(held_back(dx, far_total), x_bit)
     dy_back = exchange(held_back(dy, far_total), y_bit)
-    sums = all_sum_step(held_back(sums, dz_total), 0, core)
-    sums = all_sum_step(sums, 3 * x_bit, 0)
+    sums = all_sum_step(held_back(sums, dz_total), 3 * x_bit, 0)
     sums = all_sum_step(sums, 2 * x_bit, 0)
     sums = all_sum_step(sums, y_bit // 2, 0)
     sums = all_sum_step(sums, y_bit // 2 * 3, 0)

time: 105 us -> 105 us (level)
  waiting for transfers between devices: 42.4 us -> 44.4 us
  starting transfers between devices: 38.1 us -> 36.5 us
    ppermute x17, waiting for transfers between devices: 34.9 us -> 37.5 us  [exchange(): lax.ppermute(value, 'batch', [(s, s ^ batch_mask) for s in range(batch)])]
    ppermute x17, starting transfers between devices: 24.6 us -> 22.4 us  [exchange(): lax.ppermute(value, 'batch', [(s, s ^ batch_mask) for s in range(batch)])]
  transfers between devices with their start and end apart: 25 -> 25, of which waited for: 11 -> 10; matrix products, arithmetic and copies ran while one was open for 2% -> 2% of each run, Pallas kernels for 16% -> 16%
where the time goes in v4:
time: 105 us
  waiting for transfers between devices  44.4 us (42%)
  starting transfers between devices  36.5 us (35%)
  Pallas kernels  16.3 us (16%)
  between operations  3.4 us (3%)
  local copies, waits for them, and re-layouts  2.14 us (2%)
  other arithmetic  1.9 us (2%)
    ppermute x17, waiting for transfers between devices, exchange(): lax.ppermute(value, 'batch', [(s, s ^ batch_mask) for s in range(batch)])  37.5 us
    ppermute x17, starting transfers between devices, exchange(): lax.ppermute(value, 'batch', [(s, s ^ batch_mask) for s in range(batch)])  22.4 us
    pallas_call x5, Pallas kernels, pair_terms(): pl.pallas_call(functools.partial(pair_kernel, [len(pieces) for pieces in...  15.4 us
    ppermute x2, starting transfers between devices, exchange(): lax.ppermute(value, ('batch', 'rep'), [(s, s ^ mask) for s in range(batch...  12.8 us
    ppermute x6, waiting for transfers between devices, exchange(): return lax.ppermute(value, 'rep', [(s, s ^ rep_mask) for s in range(rep)])  6.9 us
  transfers between devices with their start and end apart: 25, of which 10 were waited for; matrix products, arithmetic and copies ran while one was open for 2% of the time, Pallas kernels for 16%

profile of v4, /device:TPU:64, one launch (start us, length us, event | category | flops | bytes accessed | tf_op | source)
XLA Modules:
  0.0 104.7 jit_solution(7452191861292145820)
XLA Ops:
  1.7 2.0 %collective-permute-start.1 = (bf16[64,1152]{1,0:T(8,128)(2,1)S(1)}, bf16[64,1152]{1,0:T(8,128)(2,1)S(1)}, u32[]{:S(2)}, u32[]{:S(2)}) collective-permute-start(bf16[64,1152]{1,0:T(8,128)(2,1)S(1)} %slice.12), channel_id=1, source_target_pairs={{0,16},{4,20},{8,24},{12,28},{16,0},{20,4},{24,8},{28,12},{32,48},... | collective-permute-start | bytes 442376 | tf_op jit(solution)/shard_map/ppermute | solution.py:23
  5.2 2.8 %collective-permute-done.1 = bf16[64,1152]{1,0:T(8,128)(2,1)S(1)} collective-permute-done((bf16[64,1152]{1,0:T(8,128)(2,1)S(1)}, bf16[64,1152]{1,0:T(8,128)(2,1)S(1)}, u32[]{:S(2)}, u32[]{:S(2)}) %collective-permute-start.1) | collective-permute-done | bytes 147488 | tf_op jit(solution)/shard_map/ppermute | solution.py:23
  8.0 5.4 %collective-permute-start.5 = (bf16[272,1152]{1,0:T(8,128)(2,1)S(1)}, bf16[272,1152]{1,0:T(8,128)(2,1)S(1)}, u32[]{:S(2)}, u32[]{:S(2)}) collective-permute-start(bf16[272,1152]{1,0:T(8,128)(2,1)S(1)} %shard_map.84.refs_1_), channel_id=1, source_target_pairs={{0,18},{1,19},{2,16},{3,17},{4,22},{5,23},{6,20},{7,21},{8,26},{9,... | collective-permute-start | bytes 1880072 | tf_op jit(solution)/shard_map/ppermute | solution.py:27
  13.4 1.5 %collective-permute-start.3 = (bf16[256,1152]{1,0:T(8,128)(2,1)S(1)}, bf16[256,1152]{1,0:T(8,128)(2,1)S(1)}, u32[]{:S(2)}, u32[]{:S(2)}) collective-permute-start(bf16[256,1152]{1,0:T(8,128)(2,1)S(1)} %copy-done), channel_id=1, source_target_pairs={{0,4},{4,0},{8,12},{12,8},{16,20},{20,16},{24,28},{28,24},{32,36},... | collective-permute-start | bytes 1769480 | tf_op jit(solution)/shard_map/ppermute | solution.py:23
  14.9 3.2 %collective-permute-start.4 = (bf16[256,1152]{1,0:T(8,128)(2,1)S(1)}, bf16[256,1152]{1,0:T(8,128)(2,1)S(1)}, u32[]{:S(2)}, u32[]{:S(2)}) collective-permute-start(bf16[256,1152]{1,0:T(8,128)(2,1)S(1)} %copy-done), channel_id=1, source_target_pairs={{0,128},{4,132},{8,136},{12,140},{16,144},{20,148},{24,152},{28,15... | collective-permute-start | bytes 1769480 | tf_op jit(solution)/shard_map/ppermute | solution.py:23
  19.6 7.7 %collective-permute-done.2 = bf16[192,1152]{1,0:T(8,128)(2,1)S(1)} collective-permute-done((bf16[192,1152]{1,0:T(8,128)(2,1)S(1)}, bf16[192,1152]{1,0:T(8,128)(2,1)S(1)}, u32[]{:S(2)}, u32[]{:S(2)}) %collective-permute-start.2) | collective-permute-done | bytes 442400 | tf_op jit(solution)/shard_map/ppermute | solution.py:23
  27.3 1.6 %collective-permute-start.7 = (bf16[256,1152]{1,0:T(8,128)(2,1)S(1)}, bf16[256,1152]{1,0:T(8,128)(2,1)S(1)}, u32[]{:S(2)}, u32[]{:S(2)}) collective-permute-start(bf16[256,1152]{1,0:T(8,128)(2,1)S(1)} %constant_dynamic-update-slice_fusion.refs_3_), channel_id=1, source_target_pairs={{0,4},{4,0},{8,12},{12,8},{16,20},{20,16},{24,28},{28,24},{32,36},... | collective-permute-start | bytes 1769480 | tf_op jit(solution)/shard_map/ppermute | solution.py:23
  28.9 3.2 %collective-permute-start.8 = (bf16[256,1152]{1,0:T(8,128)(2,1)S(1)}, bf16[256,1152]{1,0:T(8,128)(2,1)S(1)}, u32[]{:S(2)}, u32[]{:S(2)}) collective-permute-start(bf16[256,1152]{1,0:T(8,128)(2,1)S(1)} %constant_dynamic-update-slice_fusion.refs_3_), channel_id=1, source_target_pairs={{0,128},{4,132},{8,136},{12,140},{16,144},{20,148},{24,152},{28,15... | collective-permute-start | bytes 1769480 | tf_op jit(solution)/shard_map/ppermute | solution.py:23
  32.1 2.3 %shard_map.85 = (f32[256,1152]{1,0:T(8,128)S(1)}, f32[256,1152]{1,0:T(8,128)S(1)}, f32[256,1152]{1,0:T(8,128)S(1)}, f32[8,128]{1,0:T(8,128)S(1)}) custom-call(f32[2]{0:T(128)S(1)} %pad_maximum_fusion.refs_0_, bf16[272,1152]{1,0:T(8,128)(2,1)S(1)} %shard_map.84.refs_1_, bf16[272,1152]{1,0:T(8,128)(2,1)S(1)} %collective-permute-done.refs_2_, ...), custom_call_target="tpu_custom_call" | custom-call | flops 1 | bytes 1 | tf_op jit(solution)/shard_map/pallas_call | solution.py:246
  34.5 4.9 %shard_map.86 = (f32[256,1152]{1,0:T(8,128)S(1)}, bf16[256,1152]{1,0:T(8,128)(2,1)S(1)}, bf16[256,1152]{1,0:T(8,128)(2,1)S(1)}, bf16[256,1152]{1,0:T(8,128)(2,1)...) custom-call(f32[2]{0:T(128)S(1)} %pad_maximum_fusion.refs_0_, bf16[272,1152]{1,0:T(8,128)(2,1)S(1)} %shard_map.84.refs_1_, ...), custom_call_target="tpu_custom_call" | custom-call | flops 1 | bytes 1 | tf_op jit(solution)/shard_map/pallas_call | solution.py:246
  39.9 2.3 %shard_map.87 = (f32[256,1152]{1,0:T(8,128)S(1)}, f32[256,1152]{1,0:T(8,128)S(1)}, f32[256,1152]{1,0:T(8,128)S(1)}, f32[8,128]{1,0:T(8,128)S(1)}) custom-call(f32[2]{0:T(128)S(1)} %pad_maximum_fusion.refs_0_, bf16[272,1152]{1,0:T(8,128)(2,1)S(1)} %collective-permute-done.5.refs_1_, bf16[256,1152]{1,0:T(8,128)(2,1)S(1)} %copy-done, ...), custom_call_target="tpu_custom_call" | custom-call | flops 10000000000 | bytes 1 | tf_op jit(solution)/shard_map/pallas_call | solution.py:246
  42.3 2.3 %shard_map.88 = (bf16[256,1152]{1,0:T(8,128)(2,1)S(1)}, f32[256,1152]{1,0:T(8,128)S(1)}, f32[256,1152]{1,0:T(8,128)S(1)}, f32[8,128]{1,0:T(8,128)S(1)}) custom-call(f32[2]{0:T(128)S(1)} %pad_maximum_fusion.refs_0_, bf16[272,1152]{1,0:T(8,128)(2,1)S(1)} %collective-permute-done.6.refs_1_.refs_2_, bf16[256,1152]{1,0:T(8,128)(2,1)S(1)} %copy-done, ...), custom_call_target="tpu_custom_call" | custom-call | flops 1 | bytes 1 | tf_op jit(solution)/shard_map/pallas_call | solution.py:246
  44.6 3.6 %shard_map.89 = (bf16[256,1152]{1,0:T(8,128)(2,1)S(1)}, bf16[256,1152]{1,0:T(8,128)(2,1)S(1)}, f32[256,1152]{1,0:T(8,128)S(1)}, bf16[256,1152]{1,0:T(8,128)(2,1)S(1)}, f32[8,128]{1,0:T(8,128)S(1)}) custom-call(f32[2]{0:T(128)S(1)} %pad_maximum_fusion.refs_0_, bf16[272,1152]{1,0:T(8,128)(2,1)S(1)} %collective-permute-done.5.refs_1_, ...), custom_call_target="tpu_custom_call" | custom-call | flops 1 | bytes 1 | tf_op jit(solution)/shard_map/pallas_call | solution.py:246
  49.7 3.2 %collective-permute-start.14 = (bf16[256,1152]{1,0:T(8,128)(2,1)S(1)}, bf16[256,1152]{1,0:T(8,128)(2,1)S(1)}, u32[]{:S(2)}, u32[]{:S(2)}) collective-permute-start(bf16[256,1152]{1,0:T(8,128)(2,1)S(1)} %get-tuple-element.53), channel_id=1, source_target_pairs={{0,128},{4,132},{8,136},{12,140},{16,144},{20,148},{24,152},{28,15... | collective-permute-start | bytes 1769480 | tf_op jit(solution)/shard_map/ppermute | solution.py:23
  53.1 7.4 %collective-permute-start.21 = (bf16[256,1152]{1,0:T(8,128)(2,1)S(1)}, bf16[256,1152]{1,0:T(8,128)(2,1)S(1)}, u32[]{:S(2)}, u32[]{:S(2)}) collective-permute-start(bf16[256,1152]{1,0:T(8,128)(2,1)S(1)} %shard_map.93.refs_2_), channel_id=1, source_target_pairs={{0,18},{1,19},{2,16},{3,17},{4,22},{5,23},{6,20},{7,21},{8,26},{9,... | collective-permute-start | bytes 1769480 | tf_op jit(solution)/shard_map/ppermute | solution.py:27
  60.4 4.0 %collective-permute-done.11.refs_1_ = f32[8,128]{1,0:T(8,128)S(1)} collective-permute-done((f32[8,128]{1,0:T(8,128)S(1)}, f32[8,128]{1,0:T(8,128)S(1)}, u32[]{:S(2)}, u32[]{:S(2)}) %collective-permute-start.11) | collective-permute-done | bytes 4128 | tf_op jit(solution)/shard_map/ppermute | solution.py:23
  65.4 6.8 %collective-permute-done.12.refs_1_ = f32[8,128]{1,0:T(8,128)S(1)} collective-permute-done((f32[8,128]{1,0:T(8,128)S(1)}, f32[8,128]{1,0:T(8,128)S(1)}, u32[]{:S(2)}, u32[]{:S(2)}) %collective-permute-start.12) | collective-permute-done | bytes 4128 | tf_op jit(solution)/shard_map/ppermute | solution.py:25
  74.0 2.2 %collective-permute-start.15 = (f32[8,128]{1,0:T(8,128)S(1)}, f32[8,128]{1,0:T(8,128)S(1)}, u32[]{:S(2)}, u32[]{:S(2)}) collective-permute-start(f32[8,128]{1,0:T(8,128)S(1)} %shard_map.97.refs_3_.refs_0_), channel_id=1, source_target_pairs={{0,12},{4,8},{8,4},{12,0},{16,28},{20,24},{24,20},{28,16},{32,44},... | collective-permute-start | bytes 12296 | tf_op jit(solution)/shard_map/ppermute | solution.py:23
  76.3 2.7 %collective-permute-done.15.refs_1_ = f32[8,128]{1,0:T(8,128)S(1)} collective-permute-done((f32[8,128]{1,0:T(8,128)S(1)}, f32[8,128]{1,0:T(8,128)S(1)}, u32[]{:S(2)}, u32[]{:S(2)}) %collective-permute-start.15) | collective-permute-done | bytes 4128 | tf_op jit(solution)/shard_map/ppermute | solution.py:23
  78.9 1.5 %collective-permute-start.16 = (f32[8,128]{1,0:T(8,128)S(1)}, f32[8,128]{1,0:T(8,128)S(1)}, u32[]{:S(2)}, u32[]{:S(2)}) collective-permute-start(f32[8,128]{1,0:T(8,128)S(1)} %shard_map.100.refs_0_), channel_id=1, source_target_pairs={{0,8},{4,12},{8,0},{12,4},{16,24},{20,28},{24,16},{28,20},{32,40},... | collective-permute-start | bytes 12296 | tf_op jit(solution)/shard_map/ppermute | solution.py:23
  80.4 8.4 %collective-permute-done.16.refs_1_ = f32[8,128]{1,0:T(8,128)S(1)} collective-permute-done((f32[8,128]{1,0:T(8,128)S(1)}, f32[8,128]{1,0:T(8,128)S(1)}, u32[]{:S(2)}, u32[]{:S(2)}) %collective-permute-start.16) | collective-permute-done | bytes 4128 | tf_op jit(solution)/shard_map/ppermute | solution.py:23
  89.6 2.9 %collective-permute-done.17.refs_1_ = f32[8,128]{1,0:T(8,128)S(1)} collective-permute-done((f32[8,128]{1,0:T(8,128)S(1)}, f32[8,128]{1,0:T(8,128)S(1)}, u32[]{:S(2)}, u32[]{:S(2)}) %collective-permute-start.17) | collective-permute-done | bytes 4128 | tf_op jit(solution)/shard_map/ppermute | solution.py:23
  92.5 4.8 %collective-permute-done.18.refs_1_ = f32[8,128]{1,0:T(8,128)S(1)} collective-permute-done((f32[8,128]{1,0:T(8,128)S(1)}, f32[8,128]{1,0:T(8,128)S(1)}, u32[]{:S(2)}, u32[]{:S(2)}) %collective-permute-start.18) | collective-permute-done | bytes 4128 | tf_op jit(solution)/shard_map/ppermute | solution.py:23
  97.7 4.1 %collective-permute-done.19.refs_1_ = f32[8,128]{1,0:T(8,128)S(1)} collective-permute-done((f32[8,128]{1,0:T(8,128)S(1)}, f32[8,128]{1,0:T(8,128)S(1)}, u32[]{:S(2)}, u32[]{:S(2)}) %collective-permute-start.19) | collective-permute-done | bytes 4128 | tf_op jit(solution)/shard_map/ppermute | solution.py:23
  (69 shorter events, 10.5 us)
Async XLA Ops:
  1.7 6.3 %collective-permute-start.1 = (bf16[64,1152]{1,0:T(8,128)(2,1)S(1)}, bf16[64,1152]{1,0:T(8,128)(2,1)S(1)}, u32[]{:S(2)}, u32[]{:S(2)}) collective-permute-start(bf16[64,1152]{1,0:T(8,128)(2,1)S(1)} %slice.12), channel_id=1, source_target_pairs={{0,16},{4,20},{8,24},{12,28},{16,0},{20,4},{24,8},{28,12},{32,48},... | collective-permute-start | bytes 442376 | tf_op jit(solution)/shard_map/ppermute | solution.py:23
  4.7 22.5 %collective-permute-start.2 = (bf16[192,1152]{1,0:T(8,128)(2,1)S(1)}, bf16[192,1152]{1,0:T(8,128)(2,1)S(1)}, u32[]{:S(2)}, u32[]{:S(2)}) collective-permute-start(bf16[192,1152]{1,0:T(8,128)(2,1)S(1)} %slice.13), channel_id=1, source_target_pairs={{0,16},{4,20},{8,24},{12,28},{16,0},{20,4},{24,8},{28,12},{32,48},... | collective-permute-start | bytes 1327112 | tf_op jit(solution)/shard_map/ppermute | solution.py:23
  5.1 23.8 %collective-permute-start = (bf16[272,1152]{1,0:T(8,128)(2,1)S(1)}, bf16[272,1152]{1,0:T(8,128)(2,1)S(1)}, u32[]{:S(2)}, u32[]{:S(2)}) collective-permute-start(bf16[272,1152]{1,0:T(8,128)(2,1)S(1)} %shard_map.84.refs_1_), channel_id=1, source_target_pairs={{0,1},{1,0},{2,3},{3,2},{4,5},{5,4},{6,7},{7,6},{8,9},{9,8},{10,11... | collective-permute-start | bytes 1880072 | tf_op jit(solution)/shard_map/ppermute | solution.py:25
  8.0 31.4 %collective-permute-start.5 = (bf16[272,1152]{1,0:T(8,128)(2,1)S(1)}, bf16[272,1152]{1,0:T(8,128)(2,1)S(1)}, u32[]{:S(2)}, u32[]{:S(2)}) collective-permute-start(bf16[272,1152]{1,0:T(8,128)(2,1)S(1)} %shard_map.84.refs_1_), channel_id=1, source_target_pairs={{0,18},{1,19},{2,16},{3,17},{4,22},{5,23},{6,20},{7,21},{8,26},{9,... | collective-permute-start | bytes 1880072 | tf_op jit(solution)/shard_map/ppermute | solution.py:27
  13.4 21.0 %collective-permute-start.3 = (bf16[256,1152]{1,0:T(8,128)(2,1)S(1)}, bf16[256,1152]{1,0:T(8,128)(2,1)S(1)}, u32[]{:S(2)}, u32[]{:S(2)}) collective-permute-start(bf16[256,1152]{1,0:T(8,128)(2,1)S(1)} %copy-done), channel_id=1, source_target_pairs={{0,4},{4,0},{8,12},{12,8},{16,20},{20,16},{24,28},{28,24},{32,36},... | collective-permute-start | bytes 1769480 | tf_op jit(solution)/shard_map/ppermute | solution.py:23
  14.9 19.5 %collective-permute-start.4 = (bf16[256,1152]{1,0:T(8,128)(2,1)S(1)}, bf16[256,1152]{1,0:T(8,128)(2,1)S(1)}, u32[]{:S(2)}, u32[]{:S(2)}) collective-permute-start(bf16[256,1152]{1,0:T(8,128)(2,1)S(1)} %copy-done), channel_id=1, source_target_pairs={{0,128},{4,132},{8,136},{12,140},{16,144},{20,148},{24,152},{28,15... | collective-permute-start | bytes 1769480 | tf_op jit(solution)/shard_map/ppermute | solution.py:23
  27.3 17.3 %collective-permute-start.7 = (bf16[256,1152]{1,0:T(8,128)(2,1)S(1)}, bf16[256,1152]{1,0:T(8,128)(2,1)S(1)}, u32[]{:S(2)}, u32[]{:S(2)}) collective-permute-start(bf16[256,1152]{1,0:T(8,128)(2,1)S(1)} %constant_dynamic-update-slice_fusion.refs_3_), channel_id=1, source_target_pairs={{0,4},{4,0},{8,12},{12,8},{16,20},{20,16},{24,28},{28,24},{32,36},... | collective-permute-start | bytes 1769480 | tf_op jit(solution)/shard_map/ppermute | solution.py:23
  28.9 15.7 %collective-permute-start.8 = (bf16[256,1152]{1,0:T(8,128)(2,1)S(1)}, bf16[256,1152]{1,0:T(8,128)(2,1)S(1)}, u32[]{:S(2)}, u32[]{:S(2)}) collective-permute-start(bf16[256,1152]{1,0:T(8,128)(2,1)S(1)} %constant_dynamic-update-slice_fusion.refs_3_), channel_id=1, source_target_pairs={{0,128},{4,132},{8,136},{12,140},{16,144},{20,148},{24,152},{28,15... | collective-permute-start | bytes 1769480 | tf_op jit(solution)/shard_map/ppermute | solution.py:23
  39.3 25.1 %collective-permute-start.20 = (bf16[256,1152]{1,0:T(8,128)(2,1)S(1)}, bf16[256,1152]{1,0:T(8,128)(2,1)S(1)}, u32[]{:S(2)}, u32[]{:S(2)}) collective-permute-start(bf16[256,1152]{1,0:T(8,128)(2,1)S(1)} %get-tuple-element.56), channel_id=1, source_target_pairs={{0,1},{1,0},{2,3},{3,2},{4,5},{5,4},{6,7},{7,6},{8,9},{9,8},{10,11... | collective-permute-start | bytes 1769480 | tf_op jit(solution)/shard_map/ppermute | solution.py:25
  48.2 4.7 %collective-permute-start.10 = (bf16[256,1152]{1,0:T(8,128)(2,1)S(1)}, bf16[256,1152]{1,0:T(8,128)(2,1)S(1)}, u32[]{:S(2)}, u32[]{:S(2)}) collective-permute-start(bf16[256,1152]{1,0:T(8,128)(2,1)S(1)} %get-tuple-element.49), channel_id=1, source_target_pairs={{0,1},{1,0},{2,3},{3,2},{4,5},{5,4},{6,7},{7,6},{8,9},{9,8},{10,11... | collective-permute-start | bytes 1769480 | tf_op jit(solution)/shard_map/ppermute | solution.py:25
  48.5 4.3 %collective-permute-start.9 = (f32[8,128]{1,0:T(8,128)S(1)}, f32[8,128]{1,0:T(8,128)S(1)}, u32[]{:S(2)}, u32[]{:S(2)}) collective-permute-start(f32[8,128]{1,0:T(8,128)S(1)} %shard_map.90.refs_0_), channel_id=1, source_target_pairs={{0,1},{1,0},{2,3},{3,2},{4,5},{5,4},{6,7},{7,6},{8,9},{9,8},{10,11... | collective-permute-start | bytes 12296 | tf_op jit(solution)/shard_map/ppermute | solution.py:25
  48.8 24.8 %collective-permute-start.13 = (bf16[256,1152]{1,0:T(8,128)(2,1)S(1)}, bf16[256,1152]{1,0:T(8,128)(2,1)S(1)}, u32[]{:S(2)}, u32[]{:S(2)}) collective-permute-start(bf16[256,1152]{1,0:T(8,128)(2,1)S(1)} %get-tuple-element.52), channel_id=1, source_target_pairs={{0,4},{4,0},{8,12},{12,8},{16,20},{20,16},{24,28},{28,24},{32,36},... | collective-permute-start | bytes 1769480 | tf_op jit(solution)/shard_map/ppermute | solution.py:23
  49.7 24.0 %collective-permute-start.14 = (bf16[256,1152]{1,0:T(8,128)(2,1)S(1)}, bf16[256,1152]{1,0:T(8,128)(2,1)S(1)}, u32[]{:S(2)}, u32[]{:S(2)}) collective-permute-start(bf16[256,1152]{1,0:T(8,128)(2,1)S(1)} %get-tuple-element.53), channel_id=1, source_target_pairs={{0,128},{4,132},{8,136},{12,140},{16,144},{20,148},{24,152},{28,15... | collective-permute-start | bytes 1769480 | tf_op jit(solution)/shard_map/ppermute | solution.py:23
  53.1 44.3 %collective-permute-start.21 = (bf16[256,1152]{1,0:T(8,128)(2,1)S(1)}, bf16[256,1152]{1,0:T(8,128)(2,1)S(1)}, u32[]{:S(2)}, u32[]{:S(2)}) collective-permute-start(bf16[256,1152]{1,0:T(8,128)(2,1)S(1)} %shard_map.93.refs_2_), channel_id=1, source_target_pairs={{0,18},{1,19},{2,16},{3,17},{4,22},{5,23},{6,20},{7,21},{8,26},{9,... | collective-permute-start | bytes 1769480 | tf_op jit(solution)/shard_map/ppermute | solution.py:27
  60.4 4.0 %collective-permute-start.11 = (f32[8,128]{1,0:T(8,128)S(1)}, f32[8,128]{1,0:T(8,128)S(1)}, u32[]{:S(2)}, u32[]{:S(2)}) collective-permute-start(f32[8,128]{1,0:T(8,128)S(1)} %shard_map.92.refs_3_.refs_0_), channel_id=1, source_target_pairs={{0,16},{4,20},{8,24},{12,28},{16,0},{20,4},{24,8},{28,12},{32,48},... | collective-permute-start | bytes 12296 | tf_op jit(solution)/shard_map/ppermute | solution.py:23
  64.4 7.8 %collective-permute-start.12 = (f32[8,128]{1,0:T(8,128)S(1)}, f32[8,128]{1,0:T(8,128)S(1)}, u32[]{:S(2)}, u32[]{:S(2)}) collective-permute-start(f32[8,128]{1,0:T(8,128)S(1)} %shard_map.95.refs_0_), channel_id=1, source_target_pairs={{0,2},{1,3},{2,0},{3,1},{4,6},{5,7},{6,4},{7,5},{8,10},{9,11},{10,... | collective-permute-start | bytes 12296 | tf_op jit(solution)/shard_map/ppermute | solution.py:25
  64.5 33.0 %collective-permute-start.23 = (bf16[256,1152]{1,0:T(8,128)(2,1)S(1)}, bf16[256,1152]{1,0:T(8,128)(2,1)S(1)}, u32[]{:S(2)}, u32[]{:S(2)}) collective-permute-start(bf16[256,1152]{1,0:T(8,128)(2,1)S(1)} %get-tuple-element.61), channel_id=1, source_target_pairs={{0,128},{4,132},{8,136},{12,140},{16,144},{20,148},{24,152},{28,15... | collective-permute-start | bytes 1769480 | tf_op jit(solution)/shard_map/ppermute | solution.py:23
  72.3 25.3 %collective-permute-start.22 = (bf16[256,1152]{1,0:T(8,128)(2,1)S(1)}, bf16[256,1152]{1,0:T(8,128)(2,1)S(1)}, u32[]{:S(2)}, u32[]{:S(2)}) collective-permute-start(bf16[256,1152]{1,0:T(8,128)(2,1)S(1)} %get-tuple-element.59), channel_id=1, source_target_pairs={{0,4},{4,0},{8,12},{12,8},{16,20},{20,16},{24,28},{28,24},{32,36},... | collective-permute-start | bytes 1769480 | tf_op jit(solution)/shard_map/ppermute | solution.py:23
  73.9 28.6 %collective-permute-start.24 = (bf16[256,1152]{1,0:T(8,128)(2,1)S(1)}, bf16[256,1152]{1,0:T(8,128)(2,1)S(1)}, u32[]{:S(2)}, u32[]{:S(2)}) collective-permute-start(bf16[256,1152]{1,0:T(8,128)(2,1)S(1)} %shard_map.98), channel_id=1, source_target_pairs={{0,16},{4,20},{8,24},{12,28},{16,0},{20,4},{24,8},{28,12},{32,48},... | collective-permute-start | bytes 1769480 | tf_op jit(solution)/shard_map/ppermute | solution.py:23
  74.0 4.9 %collective-permute-start.15 = (f32[8,128]{1,0:T(8,128)S(1)}, f32[8,128]{1,0:T(8,128)S(1)}, u32[]{:S(2)}, u32[]{:S(2)}) collective-permute-start(f32[8,128]{1,0:T(8,128)S(1)} %shard_map.97.refs_3_.refs_0_), channel_id=1, source_target_pairs={{0,12},{4,8},{8,4},{12,0},{16,28},{20,24},{24,20},{28,16},{32,44},... | collective-permute-start | bytes 12296 | tf_op jit(solution)/shard_map/ppermute | solution.py:23
  78.9 9.9 %collective-permute-start.16 = (f32[8,128]{1,0:T(8,128)S(1)}, f32[8,128]{1,0:T(8,128)S(1)}, u32[]{:S(2)}, u32[]{:S(2)}) collective-permute-start(f32[8,128]{1,0:T(8,128)S(1)} %shard_map.100.refs_0_), channel_id=1, source_target_pairs={{0,8},{4,12},{8,0},{12,4},{16,24},{20,28},{24,16},{28,20},{32,40},... | collective-permute-start | bytes 12296 | tf_op jit(solution)/shard_map/ppermute | solution.py:23
  88.9 3.6 %collective-permute-start.17 = (f32[8,128]{1,0:T(8,128)S(1)}, f32[8,128]{1,0:T(8,128)S(1)}, u32[]{:S(2)}, u32[]{:S(2)}) collective-permute-start(f32[8,128]{1,0:T(8,128)S(1)} %shard_map.102.refs_0_), channel_id=1, source_target_pairs={{0,64},{4,68},{8,72},{12,76},{16,80},{20,84},{24,88},{28,92},{32,9... | collective-permute-start | bytes 12296 | tf_op jit(solution)/shard_map/ppermute | solution.py:23
  92.5 4.8 %collective-permute-start.18 = (f32[8,128]{1,0:T(8,128)S(1)}, f32[8,128]{1,0:T(8,128)S(1)}, u32[]{:S(2)}, u32[]{:S(2)}) collective-permute-start(f32[8,128]{1,0:T(8,128)S(1)} %shard_map.104.refs_0_), channel_id=1, source_target_pairs={{0,192},{4,196},{8,200},{12,204},{16,208},{20,212},{24,216},{28,22... | collective-permute-start | bytes 12296 | tf_op jit(solution)/shard_map/ppermute | solution.py:23
  97.3 4.5 %collective-permute-start.19 = (f32[8,128]{1,0:T(8,128)S(1)}, f32[8,128]{1,0:T(8,128)S(1)}, u32[]{:S(2)}, u32[]{:S(2)}) collective-permute-start(f32[8,128]{1,0:T(8,128)S(1)} %shard_map.106.refs_0_), channel_id=1, source_target_pairs={{0,32},{4,36},{8,40},{12,44},{16,48},{20,52},{24,56},{28,60},{32,0... | collective-permute-start | bytes 12296 | tf_op jit(solution)/shard_map/ppermute | solution.py:23
  (5 other events, 28.6 us)
